TPU v7x, 512 devices: a whole 4x8x8 slice. The times are simulated.
512 devices in a mesh: dom: 16 (over x, z_hi, core), slab: 32 (over y, z_lo).
Axes of the slice: x: 4, y: 8, z: 8 (z_hi: 2, z_lo: 4; z = z_hi * 4 + z_lo), core: 2. Of those that a mesh axis runs over, the one named last changes fastest.
Arguments:
- positions: float32 [3, 524288], P(None, ('dom', 'slab')), as said below
- features: bfloat16 [32, 524288], P(None, ('dom', 'slab')), may hold values from -6 to 6
- counts: int32 [512], P(('dom', 'slab')), may hold values from 512 to 1024, as said below
- ghost_index: int32 [512, 256], P(('dom', 'slab')), may hold values from 0 to 511, as said below
- kvec: int32 [3, 8192], replicated, may hold values from -12 to 12
- screen_len: float32 [32], replicated, may hold values from 2 to 20
- long_weight: bfloat16 [32, 32], replicated, may hold values from -1 to 1
- short_weight: bfloat16 [32, 32], replicated, may hold values from -1 to 1
Outputs:
- updated: bfloat16 [32, 524288], P(None, ('dom', 'slab'))
Inputs may be any that keep to these rules, and one draw needn't show every extreme that they name: `counts`: at least one device is full (1024 live) and at least one holds exactly 512. `ghost_index`: Lower-face senders are distinct slots below 256; upper-face senders are distinct slots from 256 to 511; all are live. `positions`: each atom lies inside its block's domain and slab region of the box.
All inputs are finite; a program needn't handle non-finite values.
Results may differ from a plain program's by a relative error of at most 0.005.
The roundings to bfloat16 on the way count: a program that leaves them out, or rounds other values in their place, can miss the bound.
Values may be sent and summed in bfloat16 or wider, within the bound.
No kernel may reach another device: no remote copies, remote signals or barrier semaphores. Data moves between devices by JAX's collectives and lax.ppermute only.
A program may use at most 128 MiB of HBM per device.

v0:
```python
import math

import jax
import jax.numpy as jnp
from jax import lax
from jax.sharding import PartitionSpec as P

box_length = 216.0
pair_scale = 12.5
short_gain = 0.5
long_gain = 16.0
table_rows = 512


def with_halo(block, sides, width):
    for axis, dim in sides:
        count = lax.axis_size(axis)
        forward = [(i, i + 1) for i in range(count - 1)]
        forward.append((count - 1, 0))
        backward = [(target, source) for source, target in forward]
        low = lax.ppermute(
            lax.slice_in_dim(block, block.shape[dim] - width, None, axis=dim), axis, forward
        )
        high = lax.ppermute(lax.slice_in_dim(block, 0, width, axis=dim), axis, backward)
        block = jnp.concatenate([low, block, high], axis=dim)
    return block


def phase_pair(kpart, coords):
    theta = (
        kpart[0][:, None] * coords[0][None, :]
        + kpart[1][:, None] * coords[1][None, :]
        + kpart[2][:, None] * coords[2][None, :]
    )
    return (jnp.cos(theta).astype(jnp.bfloat16), jnp.sin(theta).astype(jnp.bfloat16))


def phase_tables(kscaled, coords):
    total_vec = kscaled.shape[1]
    width = math.gcd(total_vec, table_rows)

    def one(index):
        kpart = lax.dynamic_slice_in_dim(kscaled, index * width, width, 1)
        return phase_pair(kpart, coords)

    cos_blocks, sin_blocks = lax.map(one, jnp.arange(total_vec // width, dtype=jnp.int32))
    return (
        cos_blocks.reshape(total_vec, coords.shape[1]),
        sin_blocks.reshape(total_vec, coords.shape[1]),
    )


def long_rows(rows, cos_part, sin_part):
    chans = rows.shape[1] // 2
    acc = lax.dot_general(
        rows[:, :chans], cos_part, (((0,), (0,)), ((), ())), preferred_element_type=jnp.float32
    )
    return acc + lax.dot_general(
        rows[:, chans:], sin_part, (((0,), (0,)), ((), ())), preferred_element_type=jnp.float32
    )


def filter_owned(summed, kscaled, screen_len, first):
    owned = lax.dynamic_slice_in_dim(kscaled, first, summed.shape[0], 1)
    ksq = owned[0] * owned[0] + owned[1] * owned[1] + owned[2] * owned[2]
    filt = 1.0 / (1.0 + ksq[:, None] * (screen_len * screen_len)[None, :])
    return (summed * jnp.concatenate([filt, filt], axis=1)).astype(jnp.bfloat16)


def local(positions, features, counts, ghost_index, kvec, screen_len, long_weight, short_weight):
    atoms = positions.shape[1]
    total_vec = kvec.shape[1]
    ghost = ghost_index.shape[1] // 2
    kscaled = kvec.astype(jnp.float32) * (2.0 * math.pi / box_length)
    valid = (lax.iota(jnp.int32, atoms) < counts[0]).astype(jnp.float32)
    masked = (features.astype(jnp.float32) * valid[None, :]).astype(jnp.bfloat16)
    export_all = jnp.concatenate([positions, masked.astype(jnp.float32)], axis=0)
    export = jnp.take(export_all, ghost_index[0], axis=1)
    extended = with_halo(export, (("dom", 1),), ghost)
    remote = jnp.concatenate([extended[:, :ghost], extended[:, 3 * ghost :]], axis=1)
    partner_pos = jnp.concatenate([positions, remote[:3]], axis=1)
    partner_feat = jnp.concatenate([masked, remote[3:].astype(jnp.bfloat16)], axis=1)
    partner_live = jnp.concatenate([valid, jnp.ones((2 * ghost,), jnp.float32)])
    squares = []
    for dim in range(3):
        diff = positions[dim][:, None] - partner_pos[dim][None, :]
        diff = diff - box_length * jnp.floor(diff / box_length + 0.5)
        squares.append(diff * diff)
    radius = squares[0] + squares[1] + squares[2]
    pair = (jnp.exp(-radius / pair_scale) * partner_live[None, :]).astype(jnp.bfloat16)
    shortmsg = lax.dot_general(
        partner_feat, pair, (((1,), (1,)), ((), ())), preferred_element_type=jnp.float32
    )
    cos_table, sin_table = phase_tables(kscaled, positions)
    real = lax.dot_general(
        cos_table, masked, (((1,), (1,)), ((), ())), preferred_element_type=jnp.float32
    )
    imag = lax.dot_general(
        sin_table, masked, (((1,), (1,)), ((), ())), preferred_element_type=jnp.float32
    )
    local_term = jnp.concatenate([real, imag], axis=1)
    owned_rows = total_vec // lax.axis_size("slab")
    partial_value = lax.psum_scatter(local_term, "slab", scatter_dimension=0, tiled=True)
    summed = lax.psum(partial_value, "dom")
    filtered = filter_owned(summed, kscaled, screen_len, lax.axis_index("slab") * owned_rows)
    longmsg = long_rows(lax.all_gather(filtered, "slab", axis=0, tiled=True), cos_table, sin_table)
    all_atoms = atoms * lax.axis_size("dom") * lax.axis_size("slab")
    long_scale = long_gain / math.sqrt(total_vec * all_atoms)
    long_mix = long_weight.astype(jnp.float32).T
    short_mix = short_weight.astype(jnp.float32).T
    mixed = (
        features.astype(jnp.float32)
        + long_scale * jnp.dot(long_mix, longmsg, precision=lax.Precision.HIGHEST)
        + short_gain * jnp.dot(short_mix, shortmsg, precision=lax.Precision.HIGHEST)
    )
    return (mixed * valid[None, :]).astype(jnp.bfloat16)


def solution(mesh):
    return jax.shard_map(
        local,
        mesh=mesh,
        in_specs=(
            P(None, ("dom", "slab")),
            P(None, ("dom", "slab")),
            P(("dom", "slab")),
            P(("dom", "slab"), None),
            P(),
            P(),
            P(),
            P(),
        ),
        out_specs=P(None, ("dom", "slab")),
        check_vma=False,
    )
```

profile of v0, /device:TPU:8, one launch (start us, length us, event | category | flops | bytes accessed | tf_op | source)
XLA Modules:
  0.0 701.0 jit_solution(14318292444047029158)
XLA Ops:
  7.2 0.9 convert_multiply_fusion.1
  8.2 184.2 %while.12 = (s32[]{:T(128)}, bf16[16,512,1024]{2,1,0:T(8,128)(2,1)}, bf16[16,512,1024]{2,1,0:T(8,128)(2,1)}, s32[16]{0:T(128)S(1)}, f32[3,8192]{1,0:T(4,128)S(1)...) while((s32[]{:T(128)}, ...), condition=%wide.region_1.2_spmd, body=%wide.region_0.1_spmd.sunk | while | flops 3670024 | bytes 2153171 | solution.py:46
  8.2 0.6 dynamic_slice.12
  9.5 0.8 fusion.65
  10.4 9.3 %fusion.66 = (bf16[16,512,1024]{2,1,0:T(8,128)(2,1)}, bf16[16,512,1024]{2,1,0:T(8,128)(2,1)}) fusion(bf16[16,512,1024]{2,1,0:T(8,128)(2,1)} %get-tuple-element.137, s32[]{:T(128)} %get-tuple-element.135, f32[1024]{0:T(1024)S(1)} %bitcast.62, f32[512]{0:T(512)S(1)} %bitcast.66, f32[1024]{0:T(1024)S(1)} %bitcast.63, f32[512]{0:T(512)S(1)} %bitcast.65, ...), kind=kLoop, calls=%fused_computation.5.clone.1 | loop fusion | flops 3670016 | bytes 2116096 | tf_op jit(solution)/shard_map/while/body/jit(dynamic_update_index_in_dim)/dynamic_update_slice | solution.py:46
  19.7 0.6 dynamic_slice.12
  21.0 0.8 fusion.65
  21.9 9.3 %fusion.66 = (bf16[16,512,1024]{2,1,0:T(8,128)(2,1)}, bf16[16,512,1024]{2,1,0:T(8,128)(2,1)}) fusion(bf16[16,512,1024]{2,1,0:T(8,128)(2,1)} %get-tuple-element.137, s32[]{:T(128)} %get-tuple-element.135, f32[1024]{0:T(1024)S(1)} %bitcast.62, f32[512]{0:T(512)S(1)} %bitcast.66, f32[1024]{0:T(1024)S(1)} %bitcast.63, f32[512]{0:T(512)S(1)} %bitcast.65, ...), kind=kLoop, calls=%fused_computation.5.clone.1 | loop fusion | flops 3670016 | bytes 2116096 | tf_op jit(solution)/shard_map/while/body/jit(dynamic_update_index_in_dim)/dynamic_update_slice | solution.py:46
  31.2 0.6 dynamic_slice.12
  32.5 0.8 fusion.65
  33.4 9.3 %fusion.66 = (bf16[16,512,1024]{2,1,0:T(8,128)(2,1)}, bf16[16,512,1024]{2,1,0:T(8,128)(2,1)}) fusion(bf16[16,512,1024]{2,1,0:T(8,128)(2,1)} %get-tuple-element.137, s32[]{:T(128)} %get-tuple-element.135, f32[1024]{0:T(1024)S(1)} %bitcast.62, f32[512]{0:T(512)S(1)} %bitcast.66, f32[1024]{0:T(1024)S(1)} %bitcast.63, f32[512]{0:T(512)S(1)} %bitcast.65, ...), kind=kLoop, calls=%fused_computation.5.clone.1 | loop fusion | flops 3670016 | bytes 2116096 | tf_op jit(solution)/shard_map/while/body/jit(dynamic_update_index_in_dim)/dynamic_update_slice | solution.py:46
  42.7 0.6 dynamic_slice.12
  44.1 0.8 fusion.65
  44.9 9.3 %fusion.66 = (bf16[16,512,1024]{2,1,0:T(8,128)(2,1)}, bf16[16,512,1024]{2,1,0:T(8,128)(2,1)}) fusion(bf16[16,512,1024]{2,1,0:T(8,128)(2,1)} %get-tuple-element.137, s32[]{:T(128)} %get-tuple-element.135, f32[1024]{0:T(1024)S(1)} %bitcast.62, f32[512]{0:T(512)S(1)} %bitcast.66, f32[1024]{0:T(1024)S(1)} %bitcast.63, f32[512]{0:T(512)S(1)} %bitcast.65, ...), kind=kLoop, calls=%fused_computation.5.clone.1 | loop fusion | flops 3670016 | bytes 2116096 | tf_op jit(solution)/shard_map/while/body/jit(dynamic_update_index_in_dim)/dynamic_update_slice | solution.py:46
  54.2 0.6 dynamic_slice.12
  55.5 0.8 fusion.65
  56.4 9.3 %fusion.66 = (bf16[16,512,1024]{2,1,0:T(8,128)(2,1)}, bf16[16,512,1024]{2,1,0:T(8,128)(2,1)}) fusion(bf16[16,512,1024]{2,1,0:T(8,128)(2,1)} %get-tuple-element.137, s32[]{:T(128)} %get-tuple-element.135, f32[1024]{0:T(1024)S(1)} %bitcast.62, f32[512]{0:T(512)S(1)} %bitcast.66, f32[1024]{0:T(1024)S(1)} %bitcast.63, f32[512]{0:T(512)S(1)} %bitcast.65, ...), kind=kLoop, calls=%fused_computation.5.clone.1 | loop fusion | flops 3670016 | bytes 2116096 | tf_op jit(solution)/shard_map/while/body/jit(dynamic_update_index_in_dim)/dynamic_update_slice | solution.py:46
  65.7 0.6 dynamic_slice.12
  67.0 0.8 fusion.65
  67.9 9.3 %fusion.66 = (bf16[16,512,1024]{2,1,0:T(8,128)(2,1)}, bf16[16,512,1024]{2,1,0:T(8,128)(2,1)}) fusion(bf16[16,512,1024]{2,1,0:T(8,128)(2,1)} %get-tuple-element.137, s32[]{:T(128)} %get-tuple-element.135, f32[1024]{0:T(1024)S(1)} %bitcast.62, f32[512]{0:T(512)S(1)} %bitcast.66, f32[1024]{0:T(1024)S(1)} %bitcast.63, f32[512]{0:T(512)S(1)} %bitcast.65, ...), kind=kLoop, calls=%fused_computation.5.clone.1 | loop fusion | flops 3670016 | bytes 2116096 | tf_op jit(solution)/shard_map/while/body/jit(dynamic_update_index_in_dim)/dynamic_update_slice | solution.py:46
  77.2 0.6 dynamic_slice.12
  78.6 0.8 fusion.65
  79.4 9.3 %fusion.66 = (bf16[16,512,1024]{2,1,0:T(8,128)(2,1)}, bf16[16,512,1024]{2,1,0:T(8,128)(2,1)}) fusion(bf16[16,512,1024]{2,1,0:T(8,128)(2,1)} %get-tuple-element.137, s32[]{:T(128)} %get-tuple-element.135, f32[1024]{0:T(1024)S(1)} %bitcast.62, f32[512]{0:T(512)S(1)} %bitcast.66, f32[1024]{0:T(1024)S(1)} %bitcast.63, f32[512]{0:T(512)S(1)} %bitcast.65, ...), kind=kLoop, calls=%fused_computation.5.clone.1 | loop fusion | flops 3670016 | bytes 2116096 | tf_op jit(solution)/shard_map/while/body/jit(dynamic_update_index_in_dim)/dynamic_update_slice | solution.py:46
  88.7 0.6 dynamic_slice.12
  90.1 0.8 fusion.65
  90.9 9.3 %fusion.66 = (bf16[16,512,1024]{2,1,0:T(8,128)(2,1)}, bf16[16,512,1024]{2,1,0:T(8,128)(2,1)}) fusion(bf16[16,512,1024]{2,1,0:T(8,128)(2,1)} %get-tuple-element.137, s32[]{:T(128)} %get-tuple-element.135, f32[1024]{0:T(1024)S(1)} %bitcast.62, f32[512]{0:T(512)S(1)} %bitcast.66, f32[1024]{0:T(1024)S(1)} %bitcast.63, f32[512]{0:T(512)S(1)} %bitcast.65, ...), kind=kLoop, calls=%fused_computation.5.clone.1 | loop fusion | flops 3670016 | bytes 2116096 | tf_op jit(solution)/shard_map/while/body/jit(dynamic_update_index_in_dim)/dynamic_update_slice | solution.py:46
  100.3 0.6 dynamic_slice.12
  101.6 0.8 fusion.65
  102.5 9.3 %fusion.66 = (bf16[16,512,1024]{2,1,0:T(8,128)(2,1)}, bf16[16,512,1024]{2,1,0:T(8,128)(2,1)}) fusion(bf16[16,512,1024]{2,1,0:T(8,128)(2,1)} %get-tuple-element.137, s32[]{:T(128)} %get-tuple-element.135, f32[1024]{0:T(1024)S(1)} %bitcast.62, f32[512]{0:T(512)S(1)} %bitcast.66, f32[1024]{0:T(1024)S(1)} %bitcast.63, f32[512]{0:T(512)S(1)} %bitcast.65, ...), kind=kLoop, calls=%fused_computation.5.clone.1 | loop fusion | flops 3670016 | bytes 2116096 | tf_op jit(solution)/shard_map/while/body/jit(dynamic_update_index_in_dim)/dynamic_update_slice | solution.py:46
  111.8 0.6 dynamic_slice.12
  113.1 0.8 fusion.65
  114.0 9.3 %fusion.66 = (bf16[16,512,1024]{2,1,0:T(8,128)(2,1)}, bf16[16,512,1024]{2,1,0:T(8,128)(2,1)}) fusion(bf16[16,512,1024]{2,1,0:T(8,128)(2,1)} %get-tuple-element.137, s32[]{:T(128)} %get-tuple-element.135, f32[1024]{0:T(1024)S(1)} %bitcast.62, f32[512]{0:T(512)S(1)} %bitcast.66, f32[1024]{0:T(1024)S(1)} %bitcast.63, f32[512]{0:T(512)S(1)} %bitcast.65, ...), kind=kLoop, calls=%fused_computation.5.clone.1 | loop fusion | flops 3670016 | bytes 2116096 | tf_op jit(solution)/shard_map/while/body/jit(dynamic_update_index_in_dim)/dynamic_update_slice | solution.py:46
  123.3 0.6 dynamic_slice.12
  124.6 0.8 fusion.65
  125.5 9.3 %fusion.66 = (bf16[16,512,1024]{2,1,0:T(8,128)(2,1)}, bf16[16,512,1024]{2,1,0:T(8,128)(2,1)}) fusion(bf16[16,512,1024]{2,1,0:T(8,128)(2,1)} %get-tuple-element.137, s32[]{:T(128)} %get-tuple-element.135, f32[1024]{0:T(1024)S(1)} %bitcast.62, f32[512]{0:T(512)S(1)} %bitcast.66, f32[1024]{0:T(1024)S(1)} %bitcast.63, f32[512]{0:T(512)S(1)} %bitcast.65, ...), kind=kLoop, calls=%fused_computation.5.clone.1 | loop fusion | flops 3670016 | bytes 2116096 | tf_op jit(solution)/shard_map/while/body/jit(dynamic_update_index_in_dim)/dynamic_update_slice | solution.py:46
  134.8 0.6 dynamic_slice.12
  136.2 0.8 fusion.65
  137.0 9.3 %fusion.66 = (bf16[16,512,1024]{2,1,0:T(8,128)(2,1)}, bf16[16,512,1024]{2,1,0:T(8,128)(2,1)}) fusion(bf16[16,512,1024]{2,1,0:T(8,128)(2,1)} %get-tuple-element.137, s32[]{:T(128)} %get-tuple-element.135, f32[1024]{0:T(1024)S(1)} %bitcast.62, f32[512]{0:T(512)S(1)} %bitcast.66, f32[1024]{0:T(1024)S(1)} %bitcast.63, f32[512]{0:T(512)S(1)} %bitcast.65, ...), kind=kLoop, calls=%fused_computation.5.clone.1 | loop fusion | flops 3670016 | bytes 2116096 | tf_op jit(solution)/shard_map/while/body/jit(dynamic_update_index_in_dim)/dynamic_update_slice | solution.py:46
  146.3 0.6 dynamic_slice.12
  147.7 0.8 fusion.65
  148.5 9.3 %fusion.66 = (bf16[16,512,1024]{2,1,0:T(8,128)(2,1)}, bf16[16,512,1024]{2,1,0:T(8,128)(2,1)}) fusion(bf16[16,512,1024]{2,1,0:T(8,128)(2,1)} %get-tuple-element.137, s32[]{:T(128)} %get-tuple-element.135, f32[1024]{0:T(1024)S(1)} %bitcast.62, f32[512]{0:T(512)S(1)} %bitcast.66, f32[1024]{0:T(1024)S(1)} %bitcast.63, f32[512]{0:T(512)S(1)} %bitcast.65, ...), kind=kLoop, calls=%fused_computation.5.clone.1 | loop fusion | flops 3670016 | bytes 2116096 | tf_op jit(solution)/shard_map/while/body/jit(dynamic_update_index_in_dim)/dynamic_update_slice | solution.py:46
  157.8 0.6 dynamic_slice.12
  159.2 0.8 fusion.65
  160.0 9.3 %fusion.66 = (bf16[16,512,1024]{2,1,0:T(8,128)(2,1)}, bf16[16,512,1024]{2,1,0:T(8,128)(2,1)}) fusion(bf16[16,512,1024]{2,1,0:T(8,128)(2,1)} %get-tuple-element.137, s32[]{:T(128)} %get-tuple-element.135, f32[1024]{0:T(1024)S(1)} %bitcast.62, f32[512]{0:T(512)S(1)} %bitcast.66, f32[1024]{0:T(1024)S(1)} %bitcast.63, f32[512]{0:T(512)S(1)} %bitcast.65, ...), kind=kLoop, calls=%fused_computation.5.clone.1 | loop fusion | flops 3670016 | bytes 2116096 | tf_op jit(solution)/shard_map/while/body/jit(dynamic_update_index_in_dim)/dynamic_update_slice | solution.py:46
  169.4 0.6 dynamic_slice.12
  170.7 0.8 fusion.65
  171.6 9.3 %fusion.66 = (bf16[16,512,1024]{2,1,0:T(8,128)(2,1)}, bf16[16,512,1024]{2,1,0:T(8,128)(2,1)}) fusion(bf16[16,512,1024]{2,1,0:T(8,128)(2,1)} %get-tuple-element.137, s32[]{:T(128)} %get-tuple-element.135, f32[1024]{0:T(1024)S(1)} %bitcast.62, f32[512]{0:T(512)S(1)} %bitcast.66, f32[1024]{0:T(1024)S(1)} %bitcast.63, f32[512]{0:T(512)S(1)} %bitcast.65, ...), kind=kLoop, calls=%fused_computation.5.clone.1 | loop fusion | flops 3670016 | bytes 2116096 | tf_op jit(solution)/shard_map/while/body/jit(dynamic_update_index_in_dim)/dynamic_update_slice | solution.py:46
  182.2 0.8 fusion.65
  183.1 9.3 %fusion.66 = (bf16[16,512,1024]{2,1,0:T(8,128)(2,1)}, bf16[16,512,1024]{2,1,0:T(8,128)(2,1)}) fusion(bf16[16,512,1024]{2,1,0:T(8,128)(2,1)} %get-tuple-element.137, s32[]{:T(128)} %get-tuple-element.135, f32[1024]{0:T(1024)S(1)} %bitcast.62, f32[512]{0:T(512)S(1)} %bitcast.66, f32[1024]{0:T(1024)S(1)} %bitcast.63, f32[512]{0:T(512)S(1)} %bitcast.65, ...), kind=kLoop, calls=%fused_computation.5.clone.1 | loop fusion | flops 3670016 | bytes 2116096 | tf_op jit(solution)/shard_map/while/body/jit(dynamic_update_index_in_dim)/dynamic_update_slice | solution.py:46
  192.4 10.9 %fusion.51 = f32[8192,32]{0,1:T(8,128)S(1)} fusion(bf16[8192,1024]{1,0:T(8,128)(2,1)} %bitcast.59, bf16[32,1024]{1,0:T(8,128)(2,1)S(1)} %get-tuple-element.56), kind=kOutput, calls=%fused_computation.84 | convolution fusion | flops 536870912 | bytes 17891328 | tf_op jit(solution)/shard_map/dot_general | solution.py:95
  203.3 5.0 fusion.52
  208.4 1.5 pad_maximum_fusion
  210.4 161.6 %reduce-scatter.2.cloned.1.call-done = f32[256,64]{0,1:T(8,128)} async-done(((f32[8192,64]{0,1:T(8,128)}), f32[256,64]{0,1:T(8,128)}) %reduce-scatter.2.cloned.1.call-update) | async-done | bytes 65552 | tf_op jit(solution)/shard_map/reduce_scatter | solution.py:103
  372.1 0.7 gather_fusion
  372.9 177.1 %all-reduce.3.cloned.1.call-done = f32[256,64]{0,1:T(8,128)} async-done(((f32[256,64]{0,1:T(8,128)}), f32[256,64]{0,1:T(8,128)}) %all-reduce.3.cloned.1.call-update) | async-done | bytes 65552 | tf_op jit(solution)/shard_map/psum | solution.py:104
  550.1 1.5 fusion.36
  551.6 1.9 collective-permute-start
  553.5 9.8 %collective-permute-start.1 = (f32[35,128]{1,0:T(8,128)S(1)}, f32[35,128]{1,0:T(8,128)S(1)}, u32[]{:S(2)}, u32[]{:S(2)}) collective-permute-start(f32[35,128]{1,0:T(8,128)S(1)} %get-tuple-element.65), channel_id=1, source_target_pairs={{32,0},{64,32},{96,64},{128,96},{160,128},{192,160},{224,192},{256... | collective-permute-start | bytes 53768 | tf_op jit(solution)/shard_map/ppermute | solution.py:24
  563.4 1.2 collective-permute-done.1
  564.7 4.8 fusion.21
  569.8 105.9 %all-gather.2.cloned.1.call-done = bf16[8192,64]{0,1:T(8,128)(2,1)} async-done(((bf16[256,64]{0,1:T(8,128)(2,1)}), bf16[8192,64]{0,1:T(8,128)(2,1)}) %all-gather.2.cloned.1.call-update) | async-done | bytes 1048592 | tf_op jit(solution)/shard_map/all_gather | solution.py:106
  675.7 9.0 %fusion.30 = f32[32,1024]{1,0:T(8,128)S(1)} fusion(bf16[8192,1024]{1,0:T(8,128)(2,1)} %bitcast.60, bf16[8192,64]{0,1:T(8,128)(2,1)} %all-gather.2.cloned.1.call-done), kind=kOutput, calls=%fused_computation.44 | convolution fusion | flops 536870912 | bytes 17432576 | tf_op jit(solution)/shard_map/dot_general | solution.py:55
  684.8 8.8 %convolution_add_fusion = f32[32,1024]{1,0:T(8,128)S(1)} fusion(f32[32,1024]{1,0:T(8,128)S(1)} %fusion.30, bf16[8192,1024]{1,0:T(8,128)(2,1)} %bitcast.57, bf16[8192,64]{0,1:T(8,128)(2,1)S(1)} %copy-done.2), kind=kOutput, calls=%fused_computation.41 | convolution fusion | flops 536903680 | bytes 17563648 | tf_op jit(solution)/shard_map/dot_general | solution.py:58
  693.6 0.9 fusion.28
  (64 shorter events, 3.0 us)
Async XLA Ops:
  6.5 563.0 %copy-start = (bf16[32,32]{1,0:T(8,128)(2,1)S(1)}, bf16[32,32]{1,0:T(8,128)(2,1)}, u32[]{:S(2)}) copy-start(bf16[32,32]{1,0:T(8,128)(2,1)} %param.17) | copy-start | bytes 6148
  6.5 365.5 %reduce-scatter.2.cloned.1.call-start = ((), (), s32[]{:S(2)}) async-start(), calls=%async_computation.1 | async-start | bytes 2162688 | tf_op jit(solution)/shard_map/reduce_scatter | solution.py:103
  8.2 184.2 %copy-start.4 = (bf16[32,1024]{1,0:T(8,128)(2,1)S(1)}, bf16[32,1024]{1,0:T(8,128)(2,1)}, u32[]{:S(2)}) copy-start(bf16[32,1024]{1,0:T(8,128)(2,1)} %param.11) | copy-start | bytes 196612
  192.4 10.9 %copy-start.1 = (bf16[16,512,1024]{2,1,0:T(8,128)(2,1)S(1)}, bf16[16,512,1024]{2,1,0:T(8,128)(2,1)}, u32[]{:S(2)}) copy-start(bf16[16,512,1024]{2,1,0:T(8,128)(2,1)} %get-tuple-element.39) | copy-start | bytes 50331652
  208.3 1.6 copy-start.3
  208.3 1.8 copy-start.7
  208.3 1.9 copy-start.6
  209.9 340.2 %all-reduce.3.cloned.1.call-start = ((), (), s32[]{:S(2)}) async-start(), calls=%async_computation.2 | async-start | bytes 131072 | tf_op jit(solution)/shard_map/psum | solution.py:104
  372.0 303.7 %all-gather.2.cloned.1.call-start = ((), (), s32[]{:S(2)}) async-start(), calls=%async_computation.3 | async-start | bytes 1081344 | tf_op jit(solution)/shard_map/all_gather | solution.py:106
  551.6 11.8 %collective-permute-start = (f32[35,128]{1,0:T(8,128)S(1)}, f32[35,128]{1,0:T(8,128)S(1)}, u32[]{:S(2)}, u32[]{:S(2)}) collective-permute-start(f32[35,128]{1,0:T(8,128)S(1)} %get-tuple-element.66), channel_id=1, source_target_pairs={{0,32},{32,64},{64,96},{96,128},{128,160},{160,192},{192,224},{224... | collective-permute-start | bytes 53768 | tf_op jit(solution)/shard_map/ppermute | solution.py:21
  553.5 11.1 %collective-permute-start.1 = (f32[35,128]{1,0:T(8,128)S(1)}, f32[35,128]{1,0:T(8,128)S(1)}, u32[]{:S(2)}, u32[]{:S(2)}) collective-permute-start(f32[35,128]{1,0:T(8,128)S(1)} %get-tuple-element.65), channel_id=1, source_target_pairs={{32,0},{64,32},{96,64},{128,96},{160,128},{192,160},{224,192},{256... | collective-permute-start | bytes 53768 | tf_op jit(solution)/shard_map/ppermute | solution.py:24
  675.7 9.0 %copy-start.2 = (bf16[8192,64]{0,1:T(8,128)(2,1)S(1)}, bf16[8192,64]{0,1:T(8,128)(2,1)}, u32[]{:S(2)}) copy-start(bf16[8192,64]{0,1:T(8,128)(2,1)} %all-gather.2.cloned.1.call-done) | copy-start | bytes 3145732
  684.8 8.8 %copy-start.5 = (bf16[32,32]{1,0:T(8,128)(2,1)S(1)}, bf16[32,32]{1,0:T(8,128)(2,1)}, u32[]{:S(2)}) copy-start(bf16[32,32]{1,0:T(8,128)(2,1)} %param.16) | copy-start | bytes 6148
Sparse Core Ops, SparseCore 0:
  210.0 161.9 reduce-scatter.1
  375.2 174.8 all-reduce.2
  552.1 123.6 all-gather.1
where the time goes:
time: 703 us; the launch traced here: 701 us
  waiting for transfers between devices  446 us (63%)
  other arithmetic  153 us (22%)
  matrix products  39.7 us (6%)
  local copies, waits for them, and re-layouts  25.8 us (4%)
  between operations  14 us (2%)
  starting transfers between devices  11.8 us (2%)
  loops' own time  10.4 us (1%)
    psum x1, waiting for transfers between devices, local(): summed = lax.psum(partial_value, 'dom')  177 us
    reduce_scatter x1, waiting for transfers between devices, local(): lax.psum_scatter(local_term, 'slab', scatter_dimension=0, tiled=True)  162 us
    dynamic_update_slice x16, other arithmetic, phase_tables(): lax.map(one, jnp.arange(total_vec // width, dtype=jnp.int32))  149 us
    all_gather x1, waiting for transfers between devices, local(): lax.all_gather(filtered, 'slab', axis=0, tiled=True)  106 us
  transfers between devices with their start and end apart: 5, of which 4 were waited for; matrix products, arithmetic and copies ran while one was open for 1% of the time, Pallas kernels for 0%

commit v1 on v0

v1 whole, which is shorter than its diff:
```python
import math

import jax
import jax.numpy as jnp
import numpy as np
from jax import lax
from jax.experimental import pallas as pl
from jax.experimental.pallas import tpu as pltpu
from jax.sharding import Mesh, PartitionSpec as P

box_length = 216.0
pair_scale = 12.5
short_gain = 0.5
long_gain = 16.0
vmem_limit = 48 * 1024 * 1024

ALL = ("x", "zh", "core", "y", "zl")
DOM = ("x", "zh", "core")
NEAR = ("x", "core")
FAR = ("zh", "y", "zl")

f32 = jnp.float32
bf16 = jnp.bfloat16


def fit_cos(degree):
    nodes = np.cos(np.pi * (np.arange(64) + 0.5) / 64)
    w = 0.125 * (nodes + 1.0)
    cheb = np.polynomial.chebyshev.Chebyshev.fit(w, np.cos(2 * np.pi * np.sqrt(w)), degree, domain=[0.0, 0.25])
    return [float(c) for c in cheb.convert(kind=np.polynomial.Polynomial).coef]


COS_POLY = fit_cos(6)


def turn_cos(v):
    r = v - jnp.floor(v + 0.5)
    w = r * r
    acc = w * COS_POLY[-1] + COS_POLY[-2]
    for c in COS_POLY[-3::-1]:
        acc = acc * w + c
    return acc


def table(coord, kind):
    row = lax.broadcasted_iota(jnp.int32, (8 if kind == "y" else 24, 1), 0)
    if kind == "x":
        freq = 4 * (row >> 3) + (row & 3) + 1
        sine = (row & 4) != 0
    elif kind == "z":
        freq = 2 * (row >> 2) + (row & 1) + 1
        sine = (row & 2) != 0
    else:
        freq = jnp.where(row < 2, 5, jnp.where(row < 4, 10, jnp.where(row < 6, 1, 2)))
        sine = (row & 1) != 0
    return turn_cos(freq.astype(f32) * (coord * (1.0 / box_length)) - jnp.where(sine, 0.25, 0.0))


def first_rows(rows):
    sub = lax.broadcasted_iota(jnp.int32, rows.shape, 0)
    return jnp.where(sub < 4, rows, jnp.where(sub == 4, 1.0, 0.0))


def wide_rows(xtab, ytab):
    groups = []
    for g in range(3):
        groups += [xtab[8 * g : 8 * g + 8] * ytab[f : f + 1] for f in range(4)]
    groups += [xtab[8 * g : 8 * g + 8] for g in range(3)]
    return groups + [first_rows(ytab)]


def tall_rows(ztab, ytab):
    sub = lax.broadcasted_iota(jnp.int32, ytab.shape, 0)
    groups = []
    for b in range(2):
        wave = jnp.where(sub < 4, ytab[4 + 2 * b : 5 + 2 * b], ytab[5 + 2 * b : 6 + 2 * b])
        for h in range(6):
            four = ztab[4 * h : 4 * h + 4]
            groups.append(jnp.concatenate([four, four], axis=0) * wave)
    groups += [ztab[8 * g : 8 * g + 8] for g in range(3)]
    return groups + [first_rows(jnp.concatenate([ytab[4:8], ytab[0:4]], axis=0))]


def store_wide(xcoord, ytab, e_ref):
    groups = wide_rows(table(xcoord, "x"), ytab)
    for n in range(0, 16, 2):
        two = jnp.concatenate(groups[n : n + 2], axis=0)
        high = two.astype(bf16)
        e_ref[8 * n : 8 * n + 16, :] = high
        e_ref[128 + 8 * n : 128 + 8 * n + 16, :] = (two - high.astype(f32)).astype(bf16)


def wide_code(lane):
    group, low = lane >> 3, lane & 7
    p = jnp.where(group < 12, 4 * (group >> 2), 4 * (group - 12)) + (low & 3) + 1
    p = jnp.where(group < 15, p, 0)
    a = jnp.where(group < 12, 1 + ((group >> 1) & 1), 0)
    a = jnp.where((group == 15) & (low < 4), 1 + (low >> 1), a)
    return p, a, lane < 125


def wide_masks(lane):
    group, low = lane >> 3, lane & 7
    m_x = jnp.where(group < 15, 4, 0)
    m_a = jnp.where(group < 12, 8, jnp.where((group == 15) & (low < 4), 1, 0))
    s_x = jnp.where((low & 4) != 0, 1.0, -1.0)
    s_a = jnp.where(jnp.where(group < 12, group & 1, low & 1) != 0, 1.0, -1.0)
    return m_x, m_a, s_x, s_a


def tall_code(group, sub):
    mixed, plain = group < 12, group < 15
    r = jnp.where(mixed, 2 * (group % 6) + (sub & 1) + 1, 4 * (group - 12) + 2 * (sub >> 2) + (sub & 1) + 1)
    r = jnp.where(plain, r, 0)
    b = jnp.where(mixed, 1 + group // 6, jnp.where(plain, 0, jnp.where(sub < 4, 1 + (sub >> 1), 0)))
    return b, r, plain | (sub < 5)


def tall_masks(group, sub):
    mixed, plain = group < 12, group < 15
    m_b = jnp.where(mixed, 4, jnp.where(plain, 0, jnp.where(sub < 4, 1, 0)))
    m_z = jnp.where(plain, 2 + 0 * sub, 0)
    s_b = jnp.where(jnp.where(mixed, sub & 4, sub & 1) != 0, 1.0, -1.0)
    s_z = jnp.where((sub & 2) != 0, 1.0, -1.0)
    return m_b, m_z, s_b, s_z


def prep_kernel(count_ref, pos_ref, feat_ref, idx_ref, pay_ref, low_ref, high_ref):
    atoms = pos_ref.shape[1]
    ghost = idx_ref.shape[1] // 2
    slot = lax.broadcasted_iota(jnp.int32, (1, atoms), 1)
    valid = (slot < count_ref[0]).astype(f32)
    masked = feat_ref[...].astype(f32) * valid
    pos = pos_ref[...]
    tail = jnp.concatenate([pos, jnp.zeros((1, atoms), f32)], axis=0)
    for g in range(pay_ref.shape[0]):
        pay_ref[g] = jnp.concatenate([masked[4 * g : 4 * g + 4], tail], axis=0)
    hi = tail.astype(bf16)
    rest = tail - hi.astype(f32)
    mid = rest.astype(bf16)
    lo = (rest - mid.astype(f32)).astype(bf16)
    table = jnp.concatenate(
        [masked.astype(bf16).astype(f32), hi.astype(f32), mid.astype(f32), lo.astype(f32), jnp.zeros((4, atoms), f32)], axis=0
    ).astype(bf16)
    half = 2 * ghost
    row = lax.broadcasted_iota(jnp.int32, (half, ghost), 0)
    for n, out in ((0, low_ref), (1, high_ref)):
        want = idx_ref[0:1, n * ghost : (n + 1) * ghost] - n * half
        pick = (row == want).astype(f32).astype(bf16)
        got = jnp.dot(table[:, n * half : (n + 1) * half], pick, preferred_element_type=f32)
        out[0:32, :] = got[0:32]
        place = (got[32:36] + got[36:40]) + got[40:44]
        out[32:40, :] = jnp.concatenate([place, jnp.zeros((4, ghost), f32)], axis=0)


def factor_kernel(in_ref, out_ref, e_ref, m_ref, acc_ref):
    step = pl.program_id(0)
    ytab = table(in_ref[0, 5:6, :], "y")
    store_wide(in_ref[0, 4:5, :], ytab, e_ref)
    groups = tall_rows(table(in_ref[0, 6:7, :], "z"), ytab)
    for c in range(4):
        line = in_ref[0, c : c + 1, :]
        for n in range(0, 16, 2):
            at = 128 * c + 8 * n
            m_ref[at : at + 16, :] = jnp.concatenate([line * groups[n], line * groups[n + 1]], axis=0).astype(bf16)
    term = lax.dot_general(m_ref[...], e_ref[...], (((1,), (1,)), ((), ())), preferred_element_type=f32)

    @pl.when(step == 0)
    def _():
        acc_ref[...] = term

    @pl.when(step > 0)
    def _():
        acc_ref[...] += term

    @pl.when(step == pl.num_programs(0) - 1)
    def _():
        for n in range(out_ref.shape[0]):
            out_ref[n] = acc_ref[8 * n : 8 * n + 8, 0:128] + acc_ref[8 * n : 8 * n + 8, 128:256]


def coef_kernel(where_ref, kvec_ref, screen_ref, out_ref):
    owner = where_ref[0]
    group = owner % 16
    chan = 4 * where_ref[1] + owner // 16

    p_c, a_c, used_c = wide_code(lax.broadcasted_iota(jnp.int32, (128, 1), 0))
    code_c = jnp.where(used_c, 4 * p_c + a_c, -1)
    b_r, r_r, used_r = tall_code(group, lax.broadcasted_iota(jnp.int32, (8, 1), 0))
    code_r = jnp.where(used_r, 4 * r_r + b_r, -1)
    width = 1024
    counts = jnp.zeros((64, 128), f32)
    for n in range(kvec_ref.shape[1] // width):
        at = slice(n * width, (n + 1) * width)
        kx, ky, kz = kvec_ref[0:1, at], kvec_ref[1:2, at], kvec_ref[2:3, at]
        size = jnp.abs(ky)
        turn = jnp.where(ky < 0, -1, 1)
        ka = jnp.where(size >= 8, 2, jnp.where(size >= 3, 1, 0))
        kb = turn * (size - 5 * ka)
        wide = jnp.where(code_c == 4 * jnp.abs(kx) + ka, 1.0, 0.0).astype(bf16)
        hit = jnp.where(code_r == 4 * jnp.abs(kz) + jnp.abs(kb), 1.0, 0.0)
        sx, sa, sb, sz = (jnp.clip(k, -1, 1).astype(f32) for k in (kx, turn * ka, kb, kz))
        signs = [sx * sa, sx * sb, sx * sz, sa * sb, sa * sz, sb * sz, (sx * sa) * (sb * sz)]
        lines = jnp.concatenate([hit] + [hit * sign for sign in signs], axis=0).astype(bf16)
        counts = counts + lax.dot_general(lines, wide, (((1,), (1,)), ((), ())), preferred_element_type=f32)
    n_0, n_xa, n_xb, n_xz, n_ab, n_az, n_bz, n_all = (counts[8 * v : 8 * v + 8] for v in range(8))

    lane = lax.broadcasted_iota(jnp.int32, (8, 128), 1)
    sub = lax.broadcasted_iota(jnp.int32, (8, 128), 0)
    p, a, used_l = wide_code(lane)
    b, r, used_s = tall_code(group, sub)
    _, _, s_x, s_a = wide_masks(lane)
    _, _, s_b, s_z = tall_masks(group, sub)
    unit = 2.0 * math.pi / box_length
    screen = unit * screen_ref[pl.ds(chan, 1), :]
    screen = screen * screen

    def filt(q):
        return 1.0 / (1.0 + (p * p + q * q + r * r).astype(f32) * screen)

    like, unlike = filt(5 * a + b), filt(5 * a - b)
    used = used_l & used_s
    mean = jnp.where(used, 0.5 * (like + unlike), 0.0)
    half = jnp.where(used, 0.5 * (like - unlike), 0.0)
    out_ref[0] = mean * n_0 + half * n_ab
    out_ref[1] = -(s_x * s_a) * (mean * n_xa + half * n_xb)
    out_ref[2] = -(s_x * s_b) * (mean * n_xb + half * n_xa)
    out_ref[3] = -(s_x * s_z) * (mean * n_xz + half * n_all)
    out_ref[4] = -(s_a * s_b) * (mean * n_ab + half * n_0)
    out_ref[5] = -(s_a * s_z) * (mean * n_az + half * n_bz)
    out_ref[6] = -(s_b * s_z) * (mean * n_bz + half * n_az)
    out_ref[7] = (s_x * s_a) * (s_b * s_z) * (mean * n_all + half * n_xz)


def owner_kernel(where_ref, part_ref, coef_ref, out_ref):
    group = where_ref[0] % 16
    totals = [part_ref[n] for n in range(4)]
    for n in range(4, part_ref.shape[0]):
        totals[n % 4] = totals[n % 4] + part_ref[n]
    total = (totals[0] + totals[1]) + (totals[2] + totals[3])
    lane = lax.broadcasted_iota(jnp.int32, (8, 128), 1)
    sub = lax.broadcasted_iota(jnp.int32, (8, 128), 0)
    m_x, m_a, _, _ = wide_masks(lane)
    m_b, m_z, _, _ = tall_masks(group, sub)

    def lanes(value, mask):
        return jnp.take_along_axis(value, lane ^ mask, axis=1)

    def rows(value, mask):
        return jnp.take_along_axis(value, sub ^ mask, axis=0)

    t_x, t_a, t_xa = lanes(total, m_x), lanes(total, m_a), lanes(total, m_x ^ m_a)
    terms = [
        total,
        t_xa,
        rows(t_x, m_b),
        rows(t_x, m_z),
        rows(t_a, m_b),
        rows(t_a, m_z),
        rows(total, m_b ^ m_z),
        rows(t_xa, m_b ^ m_z),
    ]
    done = coef_ref[0] * terms[0]
    for n in range(1, 8):
        done = done + coef_ref[n] * terms[n]
    for n in range(out_ref.shape[0]):
        out_ref[n] = done


def field_kernel(filt_ref, in_ref, out_ref, e_ref, g_ref):
    step = pl.program_id(0)

    @pl.when(step == 0)
    def _():
        for n in range(0, filt_ref.shape[0], 2):
            two = jnp.concatenate([filt_ref[n], filt_ref[n + 1]], axis=0).astype(bf16)
            g_ref[8 * n : 8 * n + 16, 0:128] = two
            g_ref[8 * n : 8 * n + 16, 128:256] = two

    ytab = table(in_ref[0, 5:6, :], "y")
    store_wide(in_ref[0, 4:5, :], ytab, e_ref)
    groups = tall_rows(table(in_ref[0, 6:7, :], "z"), ytab)
    term = jnp.dot(g_ref[...], e_ref[...], preferred_element_type=f32)
    lines = []
    for c in range(4):
        acc = term[128 * c : 128 * c + 8] * groups[0]
        for n in range(1, 16):
            acc = acc + term[128 * c + 8 * n : 128 * c + 8 * n + 8] * groups[n]
        lines.append(jnp.sum(acc, axis=0, keepdims=True))
    out_ref[0] = jnp.concatenate(lines, axis=0)


def valid_row(count_ref, atoms):
    slot = lax.broadcasted_iota(jnp.int32, (1, atoms), 1)
    return (slot < count_ref[0]).astype(f32)


def short_kernel(count_ref, pos_ref, feat_ref, g1_ref, g2_ref, out_ref):
    atoms = pos_ref.shape[1]
    masked = (feat_ref[...].astype(f32) * valid_row(count_ref, atoms)).astype(bf16)
    shrink = math.sqrt(math.log2(math.e) / pair_scale)
    box = box_length * shrink
    pos = pos_ref[...] * shrink
    xr, yr, zr = pos[0:1], pos[1:2], pos[2:3]
    pos8 = jnp.concatenate([pos, jnp.zeros((5, atoms), f32)], axis=0)

    def pairs(cols, wrap):
        dx = cols[:, 0:1] - xr
        if wrap:
            dx = jnp.abs(dx)
            dx = jnp.minimum(dx, box - dx)
        dy = cols[:, 1:2] - yr
        dz = jnp.abs(cols[:, 2:3] - zr)
        dz = jnp.minimum(dz, box - dz)
        return jnp.exp2(-(dx * dx + dy * dy + dz * dz)).astype(bf16)

    ghost = jnp.concatenate([g1_ref[...], g2_ref[...]], axis=1)
    cols = jnp.transpose(ghost[32:40] * shrink)
    short = jnp.dot(ghost[0:32].astype(bf16), pairs(cols, True), preferred_element_type=f32)
    step = 256
    for n in range(atoms // step):
        at = slice(n * step, (n + 1) * step)
        short = short + jnp.dot(masked[:, at], pairs(jnp.transpose(pos8[:, at]), False), preferred_element_type=f32)
    out_ref[...] = short


def final_kernel(count_ref, feat_ref, long_ref, short_ref, lw_ref, sw_ref, out_ref, *, long_scale):
    def mix(weight, value):
        hi = value.astype(bf16)
        lo = (value - hi.astype(f32)).astype(bf16)
        dims = (((0,), (0,)), ((), ()))
        return lax.dot_general(weight, hi, dims, preferred_element_type=f32) + lax.dot_general(
            weight, lo, dims, preferred_element_type=f32
        )

    feat = feat_ref[...].astype(f32)
    total = feat + long_scale * mix(lw_ref[...], long_ref[...]) + short_gain * mix(sw_ref[...], short_ref[...])
    out_ref[...] = (total * valid_row(count_ref, feat.shape[1])).astype(bf16)


def whole(memory=pltpu.VMEM):
    return pl.BlockSpec(memory_space=memory)


def local(positions, features, counts, ghost_index, kvec, screen_len, long_weight, short_weight):
    chans, atoms = features.shape
    total_vec = kvec.shape[1]
    ghost = ghost_index.shape[1] // 2
    near = lax.axis_size(NEAR)
    far = lax.axis_size(FAR)
    params = pltpu.CompilerParams(vmem_limit_bytes=vmem_limit)

    payload, low, high = pl.pallas_call(
        prep_kernel,
        name="prep",
        out_shape=[
            jax.ShapeDtypeStruct((near, 8, atoms), f32),
            jax.ShapeDtypeStruct((40, ghost), f32),
            jax.ShapeDtypeStruct((40, ghost), f32),
        ],
        in_specs=[whole(pltpu.SMEM), whole(), whole(), whole()],
        out_specs=[whole(), whole(), whole()],
        compiler_params=params,
    )(counts, positions, features, ghost_index)

    gathered = lax.all_to_all(payload, NEAR, 0, 0, tiled=True)
    partial = pl.pallas_call(
        factor_kernel,
        name="factor",
        grid=(near,),
        out_shape=jax.ShapeDtypeStruct((far, 8, 128), f32),
        in_specs=[pl.BlockSpec((1, 8, atoms), lambda b: (b, 0, 0))],
        out_specs=pl.BlockSpec((far, 8, 128), lambda b: (0, 0, 0)),
        scratch_shapes=[pltpu.VMEM((256, atoms), bf16), pltpu.VMEM((512, atoms), bf16), pltpu.VMEM((512, 256), f32)],
        compiler_params=params,
    )(gathered)
    place = jnp.stack([lax.axis_index(FAR), lax.axis_index(NEAR)]).astype(jnp.int32)
    screens = jnp.broadcast_to(screen_len[:, None], (chans, 128))
    partial, low, high, kvec = lax.optimization_barrier((partial, low, high, kvec))
    spread = lax.all_to_all(partial, FAR, 0, 0, tiled=True)
    core = lax.axis_index("core")
    n_dom = lax.axis_size(DOM)
    flip = [(d, d ^ 1) for d in range(n_dom)]
    step = [(d, (d + 1) % n_dom if d % 2 else (d - 1) % n_dom) for d in range(n_dom)]
    ghosts_1 = lax.ppermute(jnp.where(core == 0, high, low), DOM, flip)
    ghosts_2 = lax.ppermute(jnp.where(core == 0, low, high), DOM, step)

    coef = pl.pallas_call(
        coef_kernel,
        name="coef",
        out_shape=jax.ShapeDtypeStruct((8, 8, 128), f32),
        in_specs=[whole(pltpu.SMEM), whole(), whole()],
        out_specs=whole(),
        compiler_params=params,
        cost_estimate=pl.CostEstimate(flops=2 * 64 * 256 * total_vec, bytes_accessed=8 * total_vec, transcendentals=0),
    )(place, kvec, screens)
    short = pl.pallas_call(
        short_kernel,
        name="short",
        out_shape=jax.ShapeDtypeStruct((chans, atoms), f32),
        in_specs=[whole(pltpu.SMEM)] + [whole()] * 4,
        out_specs=whole(),
        compiler_params=params,
        cost_estimate=pl.CostEstimate(flops=2 * 256 * 1280 * atoms, bytes_accessed=10 * 32 * atoms, transcendentals=1280 * atoms),
    )(counts, positions, features, ghosts_1, ghosts_2)
    spread, coef, short = lax.optimization_barrier((spread, coef, short))
    filtered = pl.pallas_call(
        owner_kernel,
        name="owner",
        out_shape=jax.ShapeDtypeStruct((far, 8, 128), f32),
        in_specs=[whole(pltpu.SMEM), whole(), whole()],
        out_specs=whole(),
        compiler_params=params,
    )(place, spread, coef)
    everywhere = lax.all_to_all(filtered, FAR, 0, 0, tiled=True)
    field = pl.pallas_call(
        field_kernel,
        name="field",
        grid=(near,),
        out_shape=jax.ShapeDtypeStruct((near, 4, atoms), f32),
        in_specs=[
            pl.BlockSpec((far, 8, 128), lambda b: (0, 0, 0)),
            pl.BlockSpec((1, 8, atoms), lambda b: (b, 0, 0)),
        ],
        out_specs=pl.BlockSpec((1, 4, atoms), lambda b: (b, 0, 0)),
        scratch_shapes=[pltpu.VMEM((256, atoms), bf16), pltpu.VMEM((512, 256), bf16)],
        compiler_params=params,
    )(everywhere, gathered)
    longmsg = lax.all_to_all(field, NEAR, 0, 0, tiled=True).reshape(chans, atoms)
    all_atoms = atoms * lax.axis_size(ALL)
    long_scale = long_gain / math.sqrt(total_vec * all_atoms)
    return pl.pallas_call(
        lambda *refs: final_kernel(*refs, long_scale=long_scale),
        name="final",
        out_shape=jax.ShapeDtypeStruct((chans, atoms), bf16),
        in_specs=[whole(pltpu.SMEM)] + [whole()] * 5,
        out_specs=whole(),
        compiler_params=params,
    )(counts, features, longmsg, short, long_weight, short_weight)


def solution(mesh):
    fine = Mesh(mesh.devices.reshape(4, 2, 2, 8, 4), ALL)
    return jax.shard_map(
        local,
        mesh=fine,
        in_specs=(P(None, ALL), P(None, ALL), P(ALL), P(ALL, None), P(), P(), P(), P()),
        out_specs=P(None, ALL),
        check_vma=False,
    )
```

time: 703 us -> 93.4 us (0.13)
  the two profiles are of different devices: /device:TPU:8 before, /device:TPU:1 now
where the time goes in v1:
time: 93.4 us; the launch traced here: 92.9 us
  blocking collectives  48.2 us (52%)
  starting transfers between devices  23 us (25%)
  Pallas kernels  16.5 us (18%)
  local copies, waits for them, and re-layouts  2.36 us (3%)
  waiting for transfers between devices  1.94 us (2%)
    all_to_all x1, blocking collectives, local(): everywhere = lax.all_to_all(filtered, FAR, 0, 0, tiled=True)  22 us
    all_to_all x1, blocking collectives, local(): gathered = lax.all_to_all(payload, NEAR, 0, 0, tiled=True)  15.8 us
    all_to_all x1, starting transfers between devices, local(): spread = lax.all_to_all(partial, FAR, 0, 0, tiled=True)  12.6 us
    all_to_all x1, blocking collectives, local(): lax.all_to_all(field, NEAR, 0, 0, tiled=True).reshape(chans, atoms)  10.4 us
    ppermute x1, starting transfers between devices, local(): ghosts_2 = lax.ppermute(jnp.where(core == 0, low, high), DOM, step)  8.41 us
    pallas_call x1, Pallas kernels, local(): pl.pallas_call(factor_kernel, name='factor', grid=(near,), out_shape=jax....  6.08 us
    pallas_call x1, Pallas kernels, local(): pl.pallas_call(field_kernel, name='field', grid=(near,), out_shape=jax.Sh...  4.34 us
    pallas_call x1, Pallas kernels, local(): pl.pallas_call(short_kernel, name='short', out_shape=jax.ShapeDtypeStruct...  2.98 us
  transfers between devices with their start and end apart: 3, of which 1 were waited for; matrix products, arithmetic and copies ran while one was open for 0% of the time, Pallas kernels for 5%

profile of v1, /device:TPU:1, one launch (start us, length us, event | category | flops | bytes accessed | tf_op | source)
XLA Modules:
  0.0 92.9 jit_solution(992510558708901821)
XLA Ops:
  0.0 0.0 copy-start.6
  0.7 0.0 copy-done.6
  0.7 0.0 copy-start
  0.7 0.8 copy-done
  1.5 0.0 copy-start.2
  1.5 0.7 copy-done.2
  2.2 0.2 prep.1
  2.4 15.8 %all_to_all.20.in_ref = f32[8,8,1024]{2,1,0:T(8,128)S(1)} all-to-all(f32[8,8,1024]{2,1,0:T(8,128)S(1)} %get-tuple-element.15), channel_id=1, replica_groups=mesh['x'=4,'zh'=2,'core'=2,'y'=8,'zl'=4] {'x','core'}, dimensions={0} | all-to-all | bytes 524288 | tf_op jit(solution)/shard_map/all_to_all | solution.py:366
  18.2 6.1 %factor.1 = f32[64,8,128]{2,1,0:T(8,128)} custom-call(f32[8,8,1024]{2,1,0:T(8,128)S(1)} %all_to_all.20.in_ref), custom_call_target="tpu_custom_call" | custom-call | tf_op jit(solution)/shard_map/factor/pallas_call | solution.py:367
  24.3 12.6 %all-to-all-start.1 = ((f32[64,8,128]{2,1,0:T(8,128)}), f32[64,8,128]{2,1,0:T(8,128)S(1)}, u32[]{:S(2)}, u32[]{:S(2)}) async-start(f32[64,8,128]{2,1,0:T(8,128)} %factor.1), calls=%async_computation.1 | async-start | bytes 524288 | tf_op jit(solution)/shard_map/all_to_all | solution.py:380
  36.9 0.0 copy-start.7
  36.9 0.1 pad_add_fusion.where_ref
  37.0 0.0 copy-start.8
  37.0 8.4 %collective-permute-start.1 = (f32[40,128]{1,0:T(8,128)S(1)}, f32[40,128]{1,0:T(8,128)S(1)}, u32[]{:S(2)}, u32[]{:S(2)}) collective-permute-start(f32[40,128]{1,0:T(8,128)S(1)} %get-tuple-element.25), channel_id=1, source_target_pairs={{0,480},{32,64},{64,32},{96,128},{128,96},{160,192},{192,160},{224... | collective-permute-start | bytes 61448 | tf_op jit(solution)/shard_map/ppermute | solution.py:386
  45.4 1.9 %collective-permute-start = (f32[40,128]{1,0:T(8,128)S(1)}, f32[40,128]{1,0:T(8,128)S(1)}, u32[]{:S(2)}, u32[]{:S(2)}) collective-permute-start(f32[40,128]{1,0:T(8,128)S(1)} %get-tuple-element.26), channel_id=1, source_target_pairs={{0,32},{32,0},{64,96},{96,64},{128,160},{160,128},{192,224},{224,1... | collective-permute-start | bytes 61448 | tf_op jit(solution)/shard_map/ppermute | solution.py:385
  47.4 0.0 copy-done.8
  47.4 0.1 broadcast_in_dim.2.screen_ref
  47.4 0.0 copy-done.7
  47.5 0.0 copy-start.1
  47.5 0.0 copy-start.3
  47.5 1.4 %coef.1.coef_ref = f32[8,8,128]{2,1,0:T(8,128)S(1)} custom-call(s32[2]{0:T(128)S(1)} %pad_add_fusion.where_ref, s32[3,8192]{1,0:T(4,128)S(1)} %copy-done.7, f32[32,128]{1,0:T(8,128)S(1)} %broadcast_in_dim.2.screen_ref), custom_call_target="tpu_custom_call" | custom-call | flops 268435456 | bytes 65536 | tf_op jit(solution)/shard_map/coef/pallas_call | solution.py:388
  48.9 1.9 %collective-permute-done.1.g2_ref = f32[40,128]{1,0:T(8,128)S(1)} collective-permute-done((f32[40,128]{1,0:T(8,128)S(1)}, f32[40,128]{1,0:T(8,128)S(1)}, u32[]{:S(2)}, u32[]{:S(2)}) %collective-permute-start.1) | collective-permute-done | bytes 20512 | tf_op jit(solution)/shard_map/ppermute | solution.py:386
  50.8 0.0 collective-permute-done.g1_ref
  50.8 0.0 copy-done.1
  50.8 0.0 copy-done.3
  50.8 3.0 %short.1.refs_3_ = f32[32,1024]{1,0:T(8,128)S(1)} custom-call(s32[1]{0:T(128)S(6)} %copy.9.count_ref.refs_0_, f32[3,1024]{1,0:T(4,128)S(1)} %copy-done.3, bf16[32,1024]{1,0:T(8,128)(2,1)S(1)} %copy-done.1, f32[40,128]{1,0:T(8,128)S(1)} %collective-permute-done.g1_ref, f32[40,128]{1,0:T(8,128)S(1)} %collective-permute-done.1.g2_ref), custom_call_target="tpu_custom_call" | custom-call | flops 671088640 | bytes 327680 | tf_op jit(solution)/shard_map/short/pallas_call | solution.py:397
  53.8 0.0 all-to-all-done.1.part_ref
  53.8 0.7 owner.1
  54.5 22.0 %all_to_all.21.filt_ref = f32[64,8,128]{2,1,0:T(8,128)S(1)} all-to-all(f32[64,8,128]{2,1,0:T(8,128)S(1)} %owner.1), channel_id=1, replica_groups=mesh['x'=4,'zh'=2,'core'=2,'y'=8,'zl'=4] {'zh','y','zl'}, dimensions={0} | all-to-all | bytes 524288 | tf_op jit(solution)/shard_map/all_to_all | solution.py:415
  76.5 4.3 %field.1 = f32[8,4,1024]{2,1,0:T(4,128)S(1)} custom-call(f32[64,8,128]{2,1,0:T(8,128)S(1)} %all_to_all.21.filt_ref, f32[8,8,1024]{2,1,0:T(8,128)S(1)} %all_to_all.20.in_ref), custom_call_target="tpu_custom_call" | custom-call | tf_op jit(solution)/shard_map/field/pallas_call | solution.py:416
  80.9 10.4 %all_to_all.22 = f32[8,4,1024]{2,1,0:T(4,128)S(1)} all-to-all(f32[8,4,1024]{2,1,0:T(4,128)S(1)} %field.1), channel_id=1, replica_groups=mesh['x'=4,'zh'=2,'core'=2,'y'=8,'zl'=4] {'x','core'}, dimensions={0} | all-to-all | bytes 262144 | tf_op jit(solution)/shard_map/all_to_all | solution.py:429
  91.2 0.0 copy-start.4
  91.2 0.0 copy-start.5
  91.3 0.6 copy-done.4
  91.9 0.0 copy-done.5
  92.0 0.9 final.1
  (2 shorter events, 0.1 us)
Async XLA Ops:
  0.0 0.7 copy-start.6
  0.7 0.8 copy-start
  1.5 0.7 copy-start.2
  24.3 29.5 %all-to-all-start.1 = ((f32[64,8,128]{2,1,0:T(8,128)}), f32[64,8,128]{2,1,0:T(8,128)S(1)}, u32[]{:S(2)}, u32[]{:S(2)}) async-start(f32[64,8,128]{2,1,0:T(8,128)} %factor.1), calls=%async_computation.1 | async-start | bytes 524288 | tf_op jit(solution)/shard_map/all_to_all | solution.py:380
  36.9 10.5 %copy-start.7 = (s32[3,8192]{1,0:T(4,128)S(1)}, s32[3,8192]{1,0:T(4,128)}, u32[]{:S(2)}) copy-start(s32[3,8192]{1,0:T(4,128)} %kvec_ref) | copy-start | bytes 294916
  37.0 10.4 %copy-start.8 = (f32[32]{0:T(128)S(1)}, f32[32]{0:T(128)}, u32[]{:S(2)}) copy-start(f32[32]{0:T(128)} %param.13) | copy-start | bytes 388
  37.0 13.8 %collective-permute-start.1 = (f32[40,128]{1,0:T(8,128)S(1)}, f32[40,128]{1,0:T(8,128)S(1)}, u32[]{:S(2)}, u32[]{:S(2)}) collective-permute-start(f32[40,128]{1,0:T(8,128)S(1)} %get-tuple-element.25), channel_id=1, source_target_pairs={{0,480},{32,64},{64,32},{96,128},{128,96},{160,192},{192,160},{224... | collective-permute-start | bytes 61448 | tf_op jit(solution)/shard_map/ppermute | solution.py:386
  45.4 5.4 %collective-permute-start = (f32[40,128]{1,0:T(8,128)S(1)}, f32[40,128]{1,0:T(8,128)S(1)}, u32[]{:S(2)}, u32[]{:S(2)}) collective-permute-start(f32[40,128]{1,0:T(8,128)S(1)} %get-tuple-element.26), channel_id=1, source_target_pairs={{0,32},{32,0},{64,96},{96,64},{128,160},{160,128},{192,224},{224,1... | collective-permute-start | bytes 61448 | tf_op jit(solution)/shard_map/ppermute | solution.py:385
  47.5 3.4 %copy-start.1 = (bf16[32,1024]{1,0:T(8,128)(2,1)S(1)}, bf16[32,1024]{1,0:T(8,128)(2,1)}, u32[]{:S(2)}) copy-start(bf16[32,1024]{1,0:T(8,128)(2,1)} %refs_1_.1) | copy-start | bytes 196612
  47.5 3.4 %copy-start.3 = (f32[3,1024]{1,0:T(4,128)S(1)}, f32[3,1024]{1,0:T(4,128)}, u32[]{:S(2)}) copy-start(f32[3,1024]{1,0:T(4,128)} %pos_ref.3) | copy-start | bytes 36868
  91.2 0.7 copy-start.4
  91.2 0.7 copy-start.5

commit v2 on v1

v2 whole, which is shorter than its diff:
```python
import math

import jax
import jax.numpy as jnp
import numpy as np
from jax import lax
from jax.experimental import pallas as pl
from jax.experimental.pallas import tpu as pltpu
from jax.sharding import Mesh, PartitionSpec as P

box_length = 216.0
pair_scale = 12.5
short_gain = 0.5
long_gain = 16.0
vmem_limit = 48 * 1024 * 1024

ALL = ("x", "zh", "core", "y", "zl")
DOM = ("x", "zh", "core")
NEAR = ("x", "core")
FAR = ("zh", "y", "zl")

f32 = jnp.float32
bf16 = jnp.bfloat16


def fit_cos(degree):
    nodes = np.cos(np.pi * (np.arange(64) + 0.5) / 64)
    w = 0.125 * (nodes + 1.0)
    cheb = np.polynomial.chebyshev.Chebyshev.fit(w, np.cos(2 * np.pi * np.sqrt(w)), degree, domain=[0.0, 0.25])
    return [float(c) for c in cheb.convert(kind=np.polynomial.Polynomial).coef]


COS_POLY = fit_cos(6)


def turn_cos(v):
    r = v - jnp.floor(v + 0.5)
    w = r * r
    acc = w * COS_POLY[-1] + COS_POLY[-2]
    for c in COS_POLY[-3::-1]:
        acc = acc * w + c
    return acc


def table(coord, kind):
    row = lax.broadcasted_iota(jnp.int32, (8 if kind == "y" else 24, 1), 0)
    if kind == "x":
        freq = 4 * (row >> 3) + (row & 3) + 1
        sine = (row & 4) != 0
    elif kind == "z":
        freq = 2 * (row >> 2) + (row & 1) + 1
        sine = (row & 2) != 0
    else:
        freq = jnp.where(row < 2, 5, jnp.where(row < 4, 10, jnp.where(row < 6, 1, 2)))
        sine = (row & 1) != 0
    return turn_cos(freq.astype(f32) * (coord * (1.0 / box_length)) - jnp.where(sine, 0.25, 0.0))


def first_rows(rows):
    sub = lax.broadcasted_iota(jnp.int32, rows.shape, 0)
    return jnp.where(sub < 4, rows, jnp.where(sub == 4, 1.0, 0.0))


def wide_rows(xtab, ytab):
    groups = []
    for g in range(3):
        groups += [xtab[8 * g : 8 * g + 8] * ytab[f : f + 1] for f in range(4)]
    groups += [xtab[8 * g : 8 * g + 8] for g in range(3)]
    return groups + [first_rows(ytab)]


def tall_rows(ztab, ytab):
    sub = lax.broadcasted_iota(jnp.int32, ytab.shape, 0)
    groups = []
    for b in range(2):
        wave = jnp.where(sub < 4, ytab[4 + 2 * b : 5 + 2 * b], ytab[5 + 2 * b : 6 + 2 * b])
        for h in range(6):
            four = ztab[4 * h : 4 * h + 4]
            groups.append(jnp.concatenate([four, four], axis=0) * wave)
    groups += [ztab[8 * g : 8 * g + 8] for g in range(3)]
    return groups + [first_rows(jnp.concatenate([ytab[4:8], ytab[0:4]], axis=0))]


def store_wide(xcoord, ytab, e_ref, at):
    groups = wide_rows(table(xcoord, "x"), ytab)
    for n in range(0, 16, 2):
        two = jnp.concatenate(groups[n : n + 2], axis=0)
        high = two.astype(bf16)
        e_ref[8 * n : 8 * n + 16, at] = high
        e_ref[128 + 8 * n : 128 + 8 * n + 16, at] = (two - high.astype(f32)).astype(bf16)


def wide_code(lane):
    group, low = lane >> 3, lane & 7
    p = jnp.where(group < 12, 4 * (group >> 2), 4 * (group - 12)) + (low & 3) + 1
    p = jnp.where(group < 15, p, 0)
    a = jnp.where(group < 12, 1 + ((group >> 1) & 1), 0)
    a = jnp.where((group == 15) & (low < 4), 1 + (low >> 1), a)
    return p, a, lane < 125


def wide_masks(lane):
    group, low = lane >> 3, lane & 7
    m_x = jnp.where(group < 15, 4, 0)
    m_a = jnp.where(group < 12, 8, jnp.where((group == 15) & (low < 4), 1, 0))
    s_x = jnp.where((low & 4) != 0, 1.0, -1.0)
    s_a = jnp.where(jnp.where(group < 12, group & 1, low & 1) != 0, 1.0, -1.0)
    return m_x, m_a, s_x, s_a


def tall_code(group, sub):
    mixed, plain = group < 12, group < 15
    r = jnp.where(mixed, 2 * (group % 6) + (sub & 1) + 1, 4 * (group - 12) + 2 * (sub >> 2) + (sub & 1) + 1)
    r = jnp.where(plain, r, 0)
    b = jnp.where(mixed, 1 + group // 6, jnp.where(plain, 0, jnp.where(sub < 4, 1 + (sub >> 1), 0)))
    return b, r, plain | (sub < 5)


def tall_masks(group, sub):
    mixed, plain = group < 12, group < 15
    m_b = jnp.where(mixed, 4, jnp.where(plain, 0, jnp.where(sub < 4, 1, 0)))
    m_z = jnp.where(plain, 2 + 0 * sub, 0)
    s_b = jnp.where(jnp.where(mixed, sub & 4, sub & 1) != 0, 1.0, -1.0)
    s_z = jnp.where((sub & 2) != 0, 1.0, -1.0)
    return m_b, m_z, s_b, s_z


def valid_row(count_ref, atoms):
    slot = lax.broadcasted_iota(jnp.int32, (1, atoms), 1)
    return (slot < count_ref[0]).astype(f32)


def prep_kernel(count_ref, pos_hbm, feat_hbm, pay_ref, pos_ref, feat_ref, sems):
    copies = [
        pltpu.make_async_copy(feat_hbm, feat_ref, sems.at[0]),
        pltpu.make_async_copy(pos_hbm, pos_ref, sems.at[1]),
    ]
    for copy in copies:
        copy.start()
    for copy in copies:
        copy.wait()
    atoms = pos_ref.shape[1]
    masked = feat_ref[...].astype(f32) * valid_row(count_ref, atoms)
    tail = jnp.concatenate([pos_ref[...], jnp.zeros((1, atoms), f32)], axis=0)
    for g in range(pay_ref.shape[0]):
        pay_ref[g] = jnp.concatenate([masked[4 * g : 4 * g + 4], tail], axis=0)


def faces_kernel(count_ref, core_ref, pos_ref, feat_ref, idx_ref, after_ref, flip_ref, step_ref):
    del after_ref
    atoms = pos_ref.shape[1]
    ghost = idx_ref.shape[1] // 2
    masked = feat_ref[...].astype(f32) * valid_row(count_ref, atoms)
    tail = jnp.concatenate([pos_ref[...], jnp.zeros((1, atoms), f32)], axis=0)
    hi = tail.astype(bf16).astype(f32)
    mid = (tail - hi).astype(bf16).astype(f32)
    lo = (tail - hi) - mid
    parts = jnp.concatenate([masked, hi, mid, lo, jnp.zeros((4, atoms), f32)], axis=0).astype(bf16)
    half = 2 * ghost
    row = lax.broadcasted_iota(jnp.int32, (half, ghost), 0)
    faces = []
    for n in range(2):
        want = idx_ref[0:1, n * ghost : (n + 1) * ghost] - n * half
        pick = (row == want).astype(f32).astype(bf16)
        got = jnp.dot(parts[:, n * half : (n + 1) * half], pick, preferred_element_type=f32)
        place = (got[32:36] + got[36:40]) + got[40:44]
        faces.append(jnp.concatenate([got[0:32], place, jnp.zeros((4, ghost), f32)], axis=0))
    first = core_ref[0] == 0
    flip_ref[...] = jnp.where(first, faces[1], faces[0])
    step_ref[...] = jnp.where(first, faces[0], faces[1])


def factor_kernel(in_ref, out_ref, e_ref, m_ref):
    blocks, _, atoms = in_ref.shape
    total = None
    for k in range(blocks):
        cols = slice(k * atoms, (k + 1) * atoms)
        ytab = table(in_ref[k, 5:6, :], "y")
        store_wide(in_ref[k, 4:5, :], ytab, e_ref, cols)
        groups = tall_rows(table(in_ref[k, 6:7, :], "z"), ytab)
        for c in range(4):
            line = in_ref[k, c : c + 1, :]
            for n in range(0, 16, 2):
                at = 128 * c + 8 * n
                m_ref[at : at + 16, cols] = jnp.concatenate([line * groups[n], line * groups[n + 1]], axis=0).astype(bf16)
        if k % 2:
            cols = slice((k - 1) * atoms, (k + 1) * atoms)
            dims = (((1,), (1,)), ((), ()))
            term = lax.dot_general(m_ref[:, cols], e_ref[:, cols], dims, preferred_element_type=f32)
            total = term if total is None else total + term
    out_ref[...] = (total[:, 0:128] + total[:, 128:256]).astype(bf16)


def coef_kernel(where_ref, kvec_ref, screen_ref, after_ref, out_ref):
    del after_ref
    owner = where_ref[0]
    group = owner % 16
    chan = 4 * where_ref[1] + owner // 16

    p_c, a_c, used_c = wide_code(lax.broadcasted_iota(jnp.int32, (128, 1), 0))
    code_c = jnp.where(used_c, 4 * p_c + a_c, -1)
    b_r, r_r, used_r = tall_code(group, lax.broadcasted_iota(jnp.int32, (8, 1), 0))
    code_r = jnp.where(used_r, 4 * r_r + b_r, -1)
    width = 1024
    counts = jnp.zeros((64, 128), f32)
    for n in range(kvec_ref.shape[1] // width):
        at = slice(n * width, (n + 1) * width)
        kx, ky, kz = kvec_ref[0:1, at], kvec_ref[1:2, at], kvec_ref[2:3, at]
        size = jnp.abs(ky)
        turn = jnp.where(ky < 0, -1, 1)
        ka = jnp.where(size >= 8, 2, jnp.where(size >= 3, 1, 0))
        kb = turn * (size - 5 * ka)
        wide = jnp.where(code_c == 4 * jnp.abs(kx) + ka, 1.0, 0.0).astype(bf16)
        hit = jnp.where(code_r == 4 * jnp.abs(kz) + jnp.abs(kb), 1.0, 0.0)
        sx, sa, sb, sz = (jnp.clip(k, -1, 1).astype(f32) for k in (kx, turn * ka, kb, kz))
        signs = [sx * sa, sx * sb, sx * sz, sa * sb, sa * sz, sb * sz, (sx * sa) * (sb * sz)]
        lines = jnp.concatenate([hit] + [hit * sign for sign in signs], axis=0).astype(bf16)
        counts = counts + lax.dot_general(lines, wide, (((1,), (1,)), ((), ())), preferred_element_type=f32)
    n_0, n_xa, n_xb, n_xz, n_ab, n_az, n_bz, n_all = (counts[8 * v : 8 * v + 8] for v in range(8))

    lane = lax.broadcasted_iota(jnp.int32, (8, 128), 1)
    sub = lax.broadcasted_iota(jnp.int32, (8, 128), 0)
    p, a, used_l = wide_code(lane)
    b, r, used_s = tall_code(group, sub)
    _, _, s_x, s_a = wide_masks(lane)
    _, _, s_b, s_z = tall_masks(group, sub)
    unit = 2.0 * math.pi / box_length
    screen = unit * screen_ref[pl.ds(chan, 1), :]
    screen = screen * screen

    def filt(q):
        return 1.0 / (1.0 + (p * p + q * q + r * r).astype(f32) * screen)

    like, unlike = filt(5 * a + b), filt(5 * a - b)
    used = used_l & used_s
    mean = jnp.where(used, 0.5 * (like + unlike), 0.0)
    half = jnp.where(used, 0.5 * (like - unlike), 0.0)
    out_ref[0] = mean * n_0 + half * n_ab
    out_ref[1] = -(s_x * s_a) * (mean * n_xa + half * n_xb)
    out_ref[2] = -(s_x * s_b) * (mean * n_xb + half * n_xa)
    out_ref[3] = -(s_x * s_z) * (mean * n_xz + half * n_all)
    out_ref[4] = -(s_a * s_b) * (mean * n_ab + half * n_0)
    out_ref[5] = -(s_a * s_z) * (mean * n_az + half * n_bz)
    out_ref[6] = -(s_b * s_z) * (mean * n_bz + half * n_az)
    out_ref[7] = (s_x * s_a) * (s_b * s_z) * (mean * n_all + half * n_xz)


def owner_kernel(where_ref, part_ref, coef_ref, step_ref, g1_ref, out_ref, step_out):
    del g1_ref
    step_out[...] = step_ref[...]
    group = where_ref[0] % 16
    totals = [part_ref[16 * n : 16 * n + 16, :].astype(f32) for n in range(4)]
    for n in range(4, part_ref.shape[0] // 16):
        totals[n % 4] = totals[n % 4] + part_ref[16 * n : 16 * n + 16, :].astype(f32)
    total = (totals[0] + totals[1]) + (totals[2] + totals[3])
    total = total[0:8] + total[8:16]
    lane = lax.broadcasted_iota(jnp.int32, (8, 128), 1)
    sub = lax.broadcasted_iota(jnp.int32, (8, 128), 0)
    m_x, m_a, _, _ = wide_masks(lane)
    m_b, m_z, _, _ = tall_masks(group, sub)

    def lanes(value, mask):
        return jnp.take_along_axis(value, lane ^ mask, axis=1)

    def rows(value, mask):
        return jnp.take_along_axis(value, sub ^ mask, axis=0)

    t_x, t_a, t_xa = lanes(total, m_x), lanes(total, m_a), lanes(total, m_x ^ m_a)
    terms = [
        total,
        t_xa,
        rows(t_x, m_b),
        rows(t_x, m_z),
        rows(t_a, m_b),
        rows(t_a, m_z),
        rows(total, m_b ^ m_z),
        rows(t_xa, m_b ^ m_z),
    ]
    done = coef_ref[0] * terms[0]
    for n in range(1, 8):
        done = done + coef_ref[n] * terms[n]
    twice = jnp.concatenate([done, done], axis=0).astype(bf16)
    for n in range(out_ref.shape[0] // 16):
        out_ref[16 * n : 16 * n + 16, :] = twice


def field_kernel(filt_ref, in_ref, g2_ref, out_ref, e_ref, g_ref):
    del g2_ref
    g_ref[:, 0:128] = filt_ref[...]
    g_ref[:, 128:256] = filt_ref[...]
    blocks, _, atoms = out_ref.shape
    for k in range(blocks):
        cols = slice(k * atoms, (k + 1) * atoms)
        ytab = table(in_ref[k, 5:6, :], "y")
        store_wide(in_ref[k, 4:5, :], ytab, e_ref, cols)
        groups = tall_rows(table(in_ref[k, 6:7, :], "z"), ytab)
        term = jnp.dot(g_ref[...], e_ref[:, cols], preferred_element_type=f32)
        lines = []
        for c in range(4):
            acc = term[128 * c : 128 * c + 8] * groups[0]
            for n in range(1, 16):
                acc = acc + term[128 * c + 8 * n : 128 * c + 8 * n + 8] * groups[n]
            lines.append(jnp.sum(acc, axis=0, keepdims=True))
        out_ref[k] = jnp.concatenate(lines, axis=0)


shrink = math.sqrt(math.log2(math.e) / pair_scale)


def pairs(cols, rows, wrap):
    box = box_length * shrink
    dx = cols[:, 0:1] - rows[0:1]
    if wrap:
        dx = jnp.abs(dx)
        dx = jnp.minimum(dx, box - dx)
    dy = cols[:, 1:2] - rows[1:2]
    dz = jnp.abs(cols[:, 2:3] - rows[2:3])
    dz = jnp.minimum(dz, box - dz)
    return jnp.exp2(-(dx * dx + dy * dy + dz * dz)).astype(bf16)


def short_kernel(
    count_ref, pos_ref, feat_ref, g1_ref, g2_ref, lw_ref, sw_ref, after_ref, base_ref, twice_ref
):
    del after_ref
    atoms = pos_ref.shape[1]
    feat = feat_ref[...].astype(f32)
    masked = (feat * valid_row(count_ref, atoms)).astype(bf16)
    rows = pos_ref[...] * shrink
    rows8 = jnp.concatenate([rows, jnp.zeros((5, atoms), f32)], axis=0)
    ghost = jnp.concatenate([g1_ref[...], g2_ref[...]], axis=1)
    near_by = pairs(jnp.transpose(ghost[32:40] * shrink), rows, True)
    short = jnp.dot(ghost[0:32].astype(bf16), near_by, preferred_element_type=f32)
    step = 256
    for n in range(atoms // step):
        at = slice(n * step, (n + 1) * step)
        own = pairs(jnp.transpose(rows8[:, at]), rows, False)
        short = short + jnp.dot(masked[:, at], own, preferred_element_type=f32)
    mixed = jnp.dot(stacked(sw_ref[...]), split(short), preferred_element_type=f32)
    base_ref[...] = feat + short_gain * mixed
    twice_ref[...] = stacked(lw_ref[...])


def stacked(weight):
    turned = jnp.transpose(weight.astype(f32))
    return jnp.concatenate([turned, turned], axis=1).astype(bf16)


def split(value):
    high = value.astype(bf16)
    low = (value - high.astype(f32)).astype(bf16)
    return jnp.concatenate([high, low], axis=0)


def final_kernel(count_ref, base_ref, long_ref, twice_ref, out_ref, *, long_scale):
    mixed = jnp.dot(twice_ref[...], split(long_ref[...]), preferred_element_type=f32)
    total = base_ref[...] + long_scale * mixed
    out_ref[...] = (total * valid_row(count_ref, total.shape[1])).astype(bf16)


def whole(memory=pltpu.VMEM):
    return pl.BlockSpec(memory_space=memory)


def local(positions, features, counts, ghost_index, kvec, screen_len, long_weight, short_weight):
    chans, atoms = features.shape
    total_vec = kvec.shape[1]
    ghost = ghost_index.shape[1] // 2
    near = lax.axis_size(NEAR)
    far = lax.axis_size(FAR)
    params = pltpu.CompilerParams(vmem_limit_bytes=vmem_limit)

    payload = pl.pallas_call(
        prep_kernel,
        name="prep",
        out_shape=jax.ShapeDtypeStruct((near, 8, atoms), f32),
        in_specs=[whole(pltpu.SMEM), whole(pl.ANY), whole(pl.ANY)],
        out_specs=whole(),
        scratch_shapes=[
            pltpu.VMEM(positions.shape, f32),
            pltpu.VMEM(features.shape, bf16),
            pltpu.SemaphoreType.DMA((2,)),
        ],
    )(counts, positions, features)
    gathered = lax.all_to_all(payload, NEAR, 0, 0, tiled=True)

    rows = jax.ShapeDtypeStruct((8 * far, 128), bf16)

    def exchange(value):
        return lax.all_to_all(value.reshape(far, 8, 128), FAR, 0, 0, tiled=True).reshape(8 * far, 128)

    partial = pl.pallas_call(
        factor_kernel,
        name="factor",
        out_shape=rows,
        in_specs=[whole()],
        out_specs=whole(),
        scratch_shapes=[pltpu.VMEM((256, near * atoms), bf16), pltpu.VMEM((512, near * atoms), bf16)],
        compiler_params=params,
    )(gathered)
    spread = exchange(partial)

    place = jnp.stack([lax.axis_index(FAR), lax.axis_index(NEAR)]).astype(jnp.int32)
    screens = jnp.broadcast_to(screen_len[:, None], (chans, 128))
    coef = pl.pallas_call(
        coef_kernel,
        name="coef",
        out_shape=jax.ShapeDtypeStruct((8, 8, 128), f32),
        in_specs=[whole(pltpu.SMEM), whole(), whole(), whole(pl.ANY)],
        out_specs=whole(),
        compiler_params=params,
        cost_estimate=pl.CostEstimate(flops=2 * 64 * 256 * total_vec, bytes_accessed=8 * total_vec, transcendentals=0),
    )(place, kvec, screens, partial)
    core = lax.axis_index("core").reshape(1).astype(jnp.int32)
    face = jax.ShapeDtypeStruct((chans + 8, ghost), f32)
    flip_face, step_face = pl.pallas_call(
        faces_kernel,
        name="faces",
        out_shape=[face, face],
        in_specs=[whole(pltpu.SMEM), whole(pltpu.SMEM), whole(), whole(), whole(), whole(pl.ANY)],
        out_specs=[whole(), whole()],
        compiler_params=params,
    )(counts, core, positions, features, ghost_index, partial)
    n_dom = lax.axis_size(DOM)
    flip = [(d, d ^ 1) for d in range(n_dom)]
    step = [(d, (d + 1) % n_dom if d % 2 else (d - 1) % n_dom) for d in range(n_dom)]
    ghosts_1 = lax.ppermute(flip_face, DOM, flip)
    filtered, step_face = pl.pallas_call(
        owner_kernel,
        name="owner",
        out_shape=[rows, face],
        in_specs=[whole(pltpu.SMEM)] + [whole()] * 3 + [whole(pl.ANY)],
        out_specs=[whole()] * 2,
        compiler_params=params,
    )(place, spread, coef, step_face, ghosts_1)
    everywhere = exchange(filtered)
    ghosts_2 = lax.ppermute(step_face, DOM, step)
    field = pl.pallas_call(
        field_kernel,
        name="field",
        out_shape=jax.ShapeDtypeStruct((near, 4, atoms), f32),
        in_specs=[whole(), whole(), whole(pl.ANY)],
        out_specs=whole(),
        scratch_shapes=[pltpu.VMEM((256, near * atoms), bf16), pltpu.VMEM((512, 256), bf16)],
        compiler_params=params,
    )(everywhere, gathered, ghosts_2)
    base, twice = pl.pallas_call(
        short_kernel,
        name="short",
        out_shape=[jax.ShapeDtypeStruct((chans, atoms), f32), jax.ShapeDtypeStruct((chans, 2 * chans), bf16)],
        in_specs=[whole(pltpu.SMEM)] + [whole()] * 6 + [whole(pl.ANY)],
        out_specs=[whole()] * 2,
        compiler_params=params,
        cost_estimate=pl.CostEstimate(flops=2 * 256 * 1280 * atoms, bytes_accessed=10 * 32 * atoms, transcendentals=1280 * atoms),
    )(counts, positions, features, ghosts_1, ghosts_2, long_weight, short_weight, field)
    longmsg = lax.all_to_all(field, NEAR, 0, 0, tiled=True).reshape(chans, atoms)
    all_atoms = atoms * lax.axis_size(ALL)
    long_scale = long_gain / math.sqrt(total_vec * all_atoms)
    return pl.pallas_call(
        lambda *refs: final_kernel(*refs, long_scale=long_scale),
        name="final",
        out_shape=jax.ShapeDtypeStruct((chans, atoms), bf16),
        in_specs=[whole(pltpu.SMEM)] + [whole()] * 3,
        out_specs=whole(),
        compiler_params=params,
    )(counts, base, longmsg, twice)


def solution(mesh):
    fine = Mesh(mesh.devices.reshape(4, 2, 2, 8, 4), ALL)
    return jax.shard_map(
        local,
        mesh=fine,
        in_specs=(P(None, ALL), P(None, ALL), P(ALL), P(ALL, None), P(), P(), P(), P()),
        out_specs=P(None, ALL),
        check_vma=False,
    )
```

time: 93.4 us -> 83.5 us (0.89)
  blocking collectives: 48.2 us -> 16.7 us
  starting transfers between devices: 23 us -> 34.9 us
  waiting for transfers between devices: 1.94 us -> 12 us
  local copies, waits for them, and re-layouts: 2.36 us -> 0.82 us
  Pallas kernels: 16.5 us -> 17.6 us
    all_to_all x2 -> x0, blocking collectives: 32.4 us -> none  [the longest x1 22 us: local(): everywhere = lax.all_to_all(filtered, FAR, 0, 0, tiled=True)]
    all_to_all x1 -> x3, starting transfers between devices: 12.6 us -> 24.1 us  [the longest x2 18.7 us: exchange(): lax.all_to_all(value.reshape(far, 8, 128), FAR, 0, 0, tiled=True)]
    all_to_all x1 -> x3, waiting for transfers between devices: 0.01 us -> 9.84 us  [the longest x2 7.64 us: exchange(): lax.all_to_all(value.reshape(far, 8, 128), FAR, 0, 0, tiled=True)]
    unnamed x18 -> x14, local copies, waits for them, and re-layouts: 2.24 us -> 0.7 us
    pallas_call x5 -> x6, Pallas kernels: 14.2 us -> 15.4 us  [the longest x1 4.98 us: local(): pl.pallas_call(field_kernel, name='field', out_shape=jax.ShapeDtypeStruct...]
  transfers between devices with their start and end apart: 3 -> 5, of which waited for: 1 -> 4; matrix products, arithmetic and copies ran while one was open for 0% -> 0% of each run, Pallas kernels for 5% -> 6%
where the time goes in v2:
time: 83.5 us; the launch traced here: 82.9 us
  starting transfers between devices  34.9 us (42%)
  Pallas kernels  17.6 us (21%)
  blocking collectives  16.7 us (20%)
  waiting for transfers between devices  12 us (14%)
    all_to_all x2, starting transfers between devices, exchange(): lax.all_to_all(value.reshape(far, 8, 128), FAR, 0, 0, tiled=True)  18.7 us
    all_to_all x1, blocking collectives, local(): gathered = lax.all_to_all(payload, NEAR, 0, 0, tiled=True)  16.7 us
    all_to_all x2, waiting for transfers between devices, exchange(): lax.all_to_all(value.reshape(far, 8, 128), FAR, 0, 0, tiled=True)  7.64 us
    ppermute x1, starting transfers between devices, local(): ghosts_2 = lax.ppermute(step_face, DOM, step)  7.6 us
    all_to_all x1, starting transfers between devices, local(): lax.all_to_all(field, NEAR, 0, 0, tiled=True).reshape(chans, atoms)  5.36 us
    pallas_call x1, Pallas kernels, local(): pl.pallas_call(field_kernel, name='field', out_shape=jax.ShapeDtypeStruct...  4.98 us
    pallas_call x1, Pallas kernels, local(): pl.pallas_call(factor_kernel, name='factor', out_shape=rows, in_specs=[wh...  4.32 us
    ppermute x1, starting transfers between devices, local(): ghosts_1 = lax.ppermute(flip_face, DOM, flip)  3.23 us
  transfers between devices with their start and end apart: 5, of which 4 were waited for; matrix products, arithmetic and copies ran while one was open for 0% of the time, Pallas kernels for 6%

profile of v2, /device:TPU:1, one launch (start us, length us, event | category | flops | bytes accessed | tf_op | source)
XLA Modules:
  0.0 82.9 jit_solution(16458835060810315415)
XLA Ops:
  0.7 1.6 %prep.1 = f32[8,8,1024]{2,1,0:T(8,128)} custom-call(s32[1]{0:T(128)S(6)} %copy.9.count_ref.refs_0_, f32[3,1024]{1,0:T(4,128)} %pos_ref.3, bf16[32,1024]{1,0:T(8,128)(2,1)} %feat_ref.3), custom_call_target="tpu_custom_call" | custom-call | tf_op jit(solution)/shard_map/prep/pallas_call | solution.py:373
  2.2 16.7 %all_to_all.20.in_ref = f32[8,8,1024]{2,1,0:T(8,128)S(1)} all-to-all(f32[8,8,1024]{2,1,0:T(8,128)} %prep.1), channel_id=1, replica_groups=mesh['x'=4,'zh'=2,'core'=2,'y'=8,'zl'=4] {'x','core'}, dimensions={0} | all-to-all | bytes 524288 | tf_op jit(solution)/shard_map/all_to_all | solution.py:385
  18.9 4.3 %factor.1.after_ref = bf16[512,128]{1,0:T(8,128)(2,1)} custom-call(f32[8,8,1024]{2,1,0:T(8,128)S(1)} %all_to_all.20.in_ref), custom_call_target="tpu_custom_call" | custom-call | tf_op jit(solution)/shard_map/factor/pallas_call | solution.py:392
  23.3 0.0 copy-start
  23.3 0.0 copy-start.3
  23.3 12.0 %all-to-all-start.1 = ((bf16[64,8,128]{2,1,0:T(8,128)(2,1)}), bf16[64,8,128]{2,1,0:T(8,128)(2,1)S(1)}, u32[]{:S(2)}, u32[]{:S(2)}) async-start(bf16[64,8,128]{2,1,0:T(8,128)(2,1)} %bitcast.3), calls=%async_computation.1 | async-start | bytes 262144 | tf_op jit(solution)/shard_map/all_to_all | solution.py:390
  35.3 0.0 copy-start.1
  35.3 0.1 pad_add_fusion.where_ref
  35.4 0.0 copy-start.2
  35.4 0.0 copy-done
  35.4 0.6 copy-done.1
  36.0 0.1 copy-done.2
  36.1 0.2 faces.1
  36.3 0.0 copy-start.6
  36.3 3.2 %collective-permute-start = (f32[40,128]{1,0:T(8,128)S(1)}, f32[40,128]{1,0:T(8,128)S(1)}, u32[]{:S(2)}, u32[]{:S(2)}) collective-permute-start(f32[40,128]{1,0:T(8,128)S(1)} %get-tuple-element.11), channel_id=1, source_target_pairs={{0,32},{32,0},{64,96},{96,64},{128,160},{160,128},{192,224},{224,1... | collective-permute-start | bytes 61448 | tf_op jit(solution)/shard_map/ppermute | solution.py:427
  39.5 0.0 copy-done.6
  39.5 0.1 broadcast_in_dim.2.screen_ref
  39.6 0.0 copy-done.3
  39.6 1.4 %coef.1.coef_ref = f32[8,8,128]{2,1,0:T(8,128)S(1)} custom-call(s32[2]{0:T(128)S(1)} %pad_add_fusion.where_ref, s32[3,8192]{1,0:T(4,128)S(1)} %copy-done.3, f32[32,128]{1,0:T(8,128)S(1)} %broadcast_in_dim.2.screen_ref, bf16[512,128]{1,0:T(8,128)(2,1)} %factor.1.after_ref), custom_call_target="tpu_custom_call" | custom-call | flops 268435456 | bytes 65536 | tf_op jit(solution)/shard_map/coef/pallas_call | solution.py:405
  41.0 0.0 collective-permute-done.g1_ref
  41.0 5.8 %all-to-all-done.1 = bf16[64,8,128]{2,1,0:T(8,128)(2,1)S(1)} async-done(((bf16[64,8,128]{2,1,0:T(8,128)(2,1)}), bf16[64,8,128]{2,1,0:T(8,128)(2,1)S(1)}, u32[]{:S(2)}, u32[]{:S(2)}) %all-to-all-start.1) | async-done | bytes 131104 | tf_op jit(solution)/shard_map/all_to_all | solution.py:390
  46.9 1.3 %owner.1 = (bf16[512,128]{1,0:T(8,128)(2,1)}, f32[40,128]{1,0:T(8,128)S(1)}) custom-call(s32[2]{0:T(128)S(1)} %pad_add_fusion.where_ref, bf16[512,128]{1,0:T(8,128)(2,1)S(1)} %bitcast.7, f32[8,8,128]{2,1,0:T(8,128)S(1)} %coef.1.coef_ref, f32[40,128]{1,0:T(8,128)S(1)} %get-tuple-element.12.step_ref, f32[40,128]{1,0:T(8,128)S(1)} %collective-permute-done.g1_ref), custom_call_target="tpu_custom_call" | custom-call | tf_op jit(solution)/shard_map/owner/pallas_call | solution.py:428
  48.2 6.7 %all-to-all-start.2 = ((bf16[64,8,128]{2,1,0:T(8,128)(2,1)}), bf16[64,8,128]{2,1,0:T(8,128)(2,1)S(1)}, u32[]{:S(2)}, u32[]{:S(2)}) async-start(bf16[64,8,128]{2,1,0:T(8,128)(2,1)} %bitcast.5), calls=%async_computation.2 | async-start | bytes 262144 | tf_op jit(solution)/shard_map/all_to_all | solution.py:390
  54.9 7.6 %collective-permute-start.1 = (f32[40,128]{1,0:T(8,128)S(1)}, f32[40,128]{1,0:T(8,128)S(1)}, u32[]{:S(2)}, u32[]{:S(2)}) collective-permute-start(f32[40,128]{1,0:T(8,128)S(1)} %get-tuple-element.13), channel_id=1, source_target_pairs={{0,480},{32,64},{64,32},{96,128},{128,96},{160,192},{192,160},{224... | collective-permute-start | bytes 61448 | tf_op jit(solution)/shard_map/ppermute | solution.py:437
  62.5 2.1 %collective-permute-done.1.g2_ref = f32[40,128]{1,0:T(8,128)S(1)} collective-permute-done((f32[40,128]{1,0:T(8,128)S(1)}, f32[40,128]{1,0:T(8,128)S(1)}, u32[]{:S(2)}, u32[]{:S(2)}) %collective-permute-start.1) | collective-permute-done | bytes 20512 | tf_op jit(solution)/shard_map/ppermute | solution.py:437
  64.6 1.8 %all-to-all-done.2 = bf16[64,8,128]{2,1,0:T(8,128)(2,1)S(1)} async-done(((bf16[64,8,128]{2,1,0:T(8,128)(2,1)}), bf16[64,8,128]{2,1,0:T(8,128)(2,1)S(1)}, u32[]{:S(2)}, u32[]{:S(2)}) %all-to-all-start.2) | async-done | bytes 131104 | tf_op jit(solution)/shard_map/all_to_all | solution.py:390
  66.4 5.0 %field.1.after_ref = f32[8,4,1024]{2,1,0:T(4,128)} custom-call(bf16[512,128]{1,0:T(8,128)(2,1)S(1)} %bitcast.8, f32[8,8,1024]{2,1,0:T(8,128)S(1)} %all_to_all.20.in_ref, f32[40,128]{1,0:T(8,128)S(1)} %collective-permute-done.1.g2_ref), custom_call_target="tpu_custom_call" | custom-call | tf_op jit(solution)/shard_map/field/pallas_call | solution.py:438
  71.4 0.0 copy-start.4
  71.4 0.0 copy-start.5
  71.4 5.4 %all-to-all-start.3 = ((f32[8,4,1024]{2,1,0:T(4,128)}), f32[8,4,1024]{2,1,0:T(4,128)S(1)}, u32[]{:S(2)}, u32[]{:S(2)}) async-start(f32[8,4,1024]{2,1,0:T(4,128)} %field.1.after_ref), calls=%async_computation.3 | async-start | bytes 262144 | tf_op jit(solution)/shard_map/all_to_all | solution.py:456
  76.8 0.0 copy-done.4
  76.8 0.0 copy-done.5
  76.8 3.1 %short.1 = (f32[32,1024]{1,0:T(8,128)S(1)}, bf16[32,64]{1,0:T(8,128)(2,1)S(1)}) custom-call(s32[1]{0:T(128)S(6)} %copy.9.count_ref.refs_0_, f32[3,1024]{1,0:T(4,128)S(1)} %copy-done.1, bf16[32,1024]{1,0:T(8,128)(2,1)S(1)} %copy-done, f32[40,128]{1,0:T(8,128)S(1)} %collective-permute-done.g1_ref, f32[40,128]{1,0:T(8,128)S(1)} %collective-permute-done.1.g2_ref, ...), custom_call_target="tpu_custom_call" | custom-call | flops 671088640 | bytes 327680 | tf_op jit(solution)/shard_map/short/pallas_call | solution.py:447
  79.9 2.2 %all-to-all-done.3 = f32[8,4,1024]{2,1,0:T(4,128)S(1)} async-done(((f32[8,4,1024]{2,1,0:T(4,128)}), f32[8,4,1024]{2,1,0:T(4,128)S(1)}, u32[]{:S(2)}, u32[]{:S(2)}) %all-to-all-start.3) | async-done | bytes 131104 | tf_op jit(solution)/shard_map/all_to_all | solution.py:456
  82.1 0.8 final.1
  (1 shorter events, 0.0 us)
Async XLA Ops:
  23.3 12.2 %copy-start = (bf16[32,1024]{1,0:T(8,128)(2,1)S(1)}, bf16[32,1024]{1,0:T(8,128)(2,1)}, u32[]{:S(2)}) copy-start(bf16[32,1024]{1,0:T(8,128)(2,1)} %feat_ref.3) | copy-start | bytes 196612
  23.3 16.3 %copy-start.3 = (s32[3,8192]{1,0:T(4,128)S(1)}, s32[3,8192]{1,0:T(4,128)}, u32[]{:S(2)}) copy-start(s32[3,8192]{1,0:T(4,128)} %kvec_ref.1) | copy-start | bytes 294916
  23.3 23.6 %all-to-all-start.1 = ((bf16[64,8,128]{2,1,0:T(8,128)(2,1)}), bf16[64,8,128]{2,1,0:T(8,128)(2,1)S(1)}, u32[]{:S(2)}, u32[]{:S(2)}) async-start(bf16[64,8,128]{2,1,0:T(8,128)(2,1)} %bitcast.3), calls=%async_computation.1 | async-start | bytes 262144 | tf_op jit(solution)/shard_map/all_to_all | solution.py:390
  35.3 0.7 copy-start.1
  35.4 0.7 copy-start.2
  36.3 3.3 %copy-start.6 = (f32[32]{0:T(128)S(1)}, f32[32]{0:T(128)}, u32[]{:S(2)}) copy-start(f32[32]{0:T(128)} %param.13) | copy-start | bytes 388
  36.3 4.8 %collective-permute-start = (f32[40,128]{1,0:T(8,128)S(1)}, f32[40,128]{1,0:T(8,128)S(1)}, u32[]{:S(2)}, u32[]{:S(2)}) collective-permute-start(f32[40,128]{1,0:T(8,128)S(1)} %get-tuple-element.11), channel_id=1, source_target_pairs={{0,32},{32,0},{64,96},{96,64},{128,160},{160,128},{192,224},{224,1... | collective-permute-start | bytes 61448 | tf_op jit(solution)/shard_map/ppermute | solution.py:427
  48.2 18.2 %all-to-all-start.2 = ((bf16[64,8,128]{2,1,0:T(8,128)(2,1)}), bf16[64,8,128]{2,1,0:T(8,128)(2,1)S(1)}, u32[]{:S(2)}, u32[]{:S(2)}) async-start(bf16[64,8,128]{2,1,0:T(8,128)(2,1)} %bitcast.5), calls=%async_computation.2 | async-start | bytes 262144 | tf_op jit(solution)/shard_map/all_to_all | solution.py:390
  54.9 9.7 %collective-permute-start.1 = (f32[40,128]{1,0:T(8,128)S(1)}, f32[40,128]{1,0:T(8,128)S(1)}, u32[]{:S(2)}, u32[]{:S(2)}) collective-permute-start(f32[40,128]{1,0:T(8,128)S(1)} %get-tuple-element.13), channel_id=1, source_target_pairs={{0,480},{32,64},{64,32},{96,128},{128,96},{160,192},{192,160},{224... | collective-permute-start | bytes 61448 | tf_op jit(solution)/shard_map/ppermute | solution.py:437
  71.4 5.4 %copy-start.4 = (bf16[32,32]{1,0:T(8,128)(2,1)S(1)}, bf16[32,32]{1,0:T(8,128)(2,1)}, u32[]{:S(2)}) copy-start(bf16[32,32]{1,0:T(8,128)(2,1)} %lw_ref.1) | copy-start | bytes 6148
  71.4 5.4 %copy-start.5 = (bf16[32,32]{1,0:T(8,128)(2,1)S(1)}, bf16[32,32]{1,0:T(8,128)(2,1)}, u32[]{:S(2)}) copy-start(bf16[32,32]{1,0:T(8,128)(2,1)} %sw_ref.1) | copy-start | bytes 6148
  71.4 10.7 %all-to-all-start.3 = ((f32[8,4,1024]{2,1,0:T(4,128)}), f32[8,4,1024]{2,1,0:T(4,128)S(1)}, u32[]{:S(2)}, u32[]{:S(2)}) async-start(f32[8,4,1024]{2,1,0:T(4,128)} %field.1.after_ref), calls=%async_computation.3 | async-start | bytes 262144 | tf_op jit(solution)/shard_map/all_to_all | solution.py:456

commit v3 on v2

--- a/solution.py
+++ b/solution.py
@@ -12,6 +12,11 @@
 pair_scale = 12.5
 short_gain = 0.5
 long_gain = 16.0
+feature_top = 6.0
+feature_steps = 32767.0
+first_in = 59
+first_out = 59
+first_near = 4
 vmem_limit = 48 * 1024 * 1024
 
 ALL = ("x", "zh", "core", "y", "zl")
@@ -42,7 +47,7 @@
     return acc
 
 
-def table(coord, kind):
+def table(turns, kind):
     row = lax.broadcasted_iota(jnp.int32, (8 if kind == "y" else 24, 1), 0)
     if kind == "x":
         freq = 4 * (row >> 3) + (row & 3) + 1
@@ -53,7 +58,7 @@
     else:
         freq = jnp.where(row < 2, 5, jnp.where(row < 4, 10, jnp.where(row < 6, 1, 2)))
         sine = (row & 1) != 0
-    return turn_cos(freq.astype(f32) * (coord * (1.0 / box_length)) - jnp.where(sine, 0.25, 0.0))
+    return turn_cos(freq.astype(f32) * turns - jnp.where(sine, 0.25, 0.0))
 
 
 def first_rows(rows):
@@ -81,8 +86,8 @@
     return groups + [first_rows(jnp.concatenate([ytab[4:8], ytab[0:4]], axis=0))]
 
 
-def store_wide(xcoord, ytab, e_ref, at):
-    groups = wide_rows(table(xcoord, "x"), ytab)
+def store_wide(xturns, ytab, e_ref, at):
+    groups = wide_rows(table(xturns, "x"), ytab)
     for n in range(0, 16, 2):
         two = jnp.concatenate(groups[n : n + 2], axis=0)
         high = two.astype(bf16)
@@ -141,9 +146,23 @@
         copy.wait()
     atoms = pos_ref.shape[1]
     masked = feat_ref[...].astype(f32) * valid_row(count_ref, atoms)
-    tail = jnp.concatenate([pos_ref[...], jnp.zeros((1, atoms), f32)], axis=0)
+    level = jnp.floor(masked * (feature_steps / feature_top) + 0.5).astype(jnp.int32)
+    below = jnp.concatenate([level[2:], level[:2]], axis=0)
+    words = (level << 16) | (below & 0xFFFF)
+    x, y, z = (
+        jnp.clip(jnp.floor(pos_ref[i : i + 1, :] * (2.0**bits / box_length) + 0.5).astype(jnp.int32), 0, 2**bits - 1)
+        for i, bits in enumerate((21, 21, 22))
+    )
+    place = jnp.concatenate([(x << 11) | (y >> 10), ((y & 1023) << 22) | z], axis=0)
     for g in range(pay_ref.shape[0]):
-        pay_ref[g] = jnp.concatenate([masked[4 * g : 4 * g + 4], tail], axis=0)
+        pay_ref[g] = jnp.concatenate([words[4 * g : 4 * g + 2], place], axis=0)
+
+
+def unpack_turns(in_ref, turns_ref):
+    first, second = in_ref[:, 2, :], in_ref[:, 3, :]
+    turns_ref[0] = lax.shift_right_logical(first, 11).astype(f32) * 2.0**-21
+    turns_ref[1] = (((first & 2047) << 10) | lax.shift_right_logical(second, 22)).astype(f32) * 2.0**-21
+    turns_ref[2] = (second & (2**22 - 1)).astype(f32) * 2.0**-22
 
 
 def faces_kernel(count_ref, core_ref, pos_ref, feat_ref, idx_ref, after_ref, flip_ref, step_ref):
@@ -170,16 +189,21 @@
     step_ref[...] = jnp.where(first, faces[0], faces[1])
 
 
-def factor_kernel(in_ref, out_ref, e_ref, m_ref):
+def factor_kernel(in_ref, out_ref, e_ref, m_ref, turns_ref, line_ref):
     blocks, _, atoms = in_ref.shape
+    unpack_turns(in_ref, turns_ref)
+    for i in range(2):
+        word = in_ref[:, i, :]
+        line_ref[i] = (word >> 16).astype(f32) * (feature_top / feature_steps)
+        line_ref[2 + i] = ((word << 16) >> 16).astype(f32) * (feature_top / feature_steps)
     total = None
     for k in range(blocks):
         cols = slice(k * atoms, (k + 1) * atoms)
-        ytab = table(in_ref[k, 5:6, :], "y")
-        store_wide(in_ref[k, 4:5, :], ytab, e_ref, cols)
-        groups = tall_rows(table(in_ref[k, 6:7, :], "z"), ytab)
+        ytab = table(turns_ref[1, k : k + 1, :], "y")
+        store_wide(turns_ref[0, k : k + 1, :], ytab, e_ref, cols)
+        groups = tall_rows(table(turns_ref[2, k : k + 1, :], "z"), ytab)
         for c in range(4):
-            line = in_ref[k, c : c + 1, :]
+            line = line_ref[c, k : k + 1, :]
             for n in range(0, 16, 2):
                 at = 128 * c + 8 * n
                 m_ref[at : at + 16, cols] = jnp.concatenate([line * groups[n], line * groups[n + 1]], axis=0).astype(bf16)
@@ -284,16 +308,20 @@
         out_ref[16 * n : 16 * n + 16, :] = twice
 
 
-def field_kernel(filt_ref, in_ref, g2_ref, out_ref, e_ref, g_ref):
-    del g2_ref
-    g_ref[:, 0:128] = filt_ref[...]
-    g_ref[:, 128:256] = filt_ref[...]
-    blocks, _, atoms = out_ref.shape
-    for k in range(blocks):
-        cols = slice(k * atoms, (k + 1) * atoms)
-        ytab = table(in_ref[k, 5:6, :], "y")
-        store_wide(in_ref[k, 4:5, :], ytab, e_ref, cols)
-        groups = tall_rows(table(in_ref[k, 6:7, :], "z"), ytab)
+def field_blocks(first, filt_ref, in_ref, out_ref, e_ref, g_ref, turns_ref):
+    unpack_turns(in_ref, turns_ref)
+    rows = filt_ref.shape[0]
+    late = 8 * (first_out - first_in) % rows
+    for at in (0, 128):
+        g_ref[late:rows, at : at + 128] = filt_ref[0 : rows - late, :]
+        if late:
+            g_ref[0:late, at : at + 128] = filt_ref[rows - late : rows, :]
+    atoms = out_ref.shape[2]
+    for k in range(first, out_ref.shape[0]):
+        cols = slice((k - first) * atoms, (k - first + 1) * atoms)
+        ytab = table(turns_ref[1, k : k + 1, :], "y")
+        store_wide(turns_ref[0, k : k + 1, :], ytab, e_ref, cols)
+        groups = tall_rows(table(turns_ref[2, k : k + 1, :], "z"), ytab)
         term = jnp.dot(g_ref[...], e_ref[:, cols], preferred_element_type=f32)
         lines = []
         for c in range(4):
@@ -302,6 +330,17 @@
                 acc = acc + term[128 * c + 8 * n : 128 * c + 8 * n + 8] * groups[n]
             lines.append(jnp.sum(acc, axis=0, keepdims=True))
         out_ref[k] = jnp.concatenate(lines, axis=0)
+
+
+def field_kernel(filt_ref, in_ref, out_ref, e_ref, g_ref, turns_ref):
+    field_blocks(0, filt_ref, in_ref, out_ref, e_ref, g_ref, turns_ref)
+
+
+def rest_kernel(filt_ref, in_ref, part_ref, g2_ref, out_ref, e_ref, g_ref, turns_ref):
+    del g2_ref
+    done = part_ref.shape[0]
+    out_ref[0:done] = part_ref[...]
+    field_blocks(done, filt_ref, in_ref, out_ref, e_ref, g_ref, turns_ref)
 
 
 shrink = math.sqrt(math.log2(math.e) / pair_scale)
@@ -358,6 +397,12 @@
     out_ref[...] = (total * valid_row(count_ref, total.shape[1])).astype(bf16)
 
 
+def swap_parts(parts, axis, first):
+    count = parts.shape[0]
+    order = [[(n + first) % count for n in range(count)]]
+    return lax.all_to_all(parts, axis, 0, 0, axis_index_groups=order, tiled=True)
+
+
 def whole(memory=pltpu.VMEM):
     return pl.BlockSpec(memory_space=memory)
 
@@ -373,7 +418,7 @@
     payload = pl.pallas_call(
         prep_kernel,
         name="prep",
-        out_shape=jax.ShapeDtypeStruct((near, 8, atoms), f32),
+        out_shape=jax.ShapeDtypeStruct((near, 4, atoms), jnp.int32),
         in_specs=[whole(pltpu.SMEM), whole(pl.ANY), whole(pl.ANY)],
         out_specs=whole(),
         scratch_shapes=[
@@ -382,12 +427,13 @@
             pltpu.SemaphoreType.DMA((2,)),
         ],
     )(counts, positions, features)
-    gathered = lax.all_to_all(payload, NEAR, 0, 0, tiled=True)
+    gathered = swap_parts(payload, NEAR, first_near)
 
     rows = jax.ShapeDtypeStruct((8 * far, 128), bf16)
 
-    def exchange(value):
-        return lax.all_to_all(value.reshape(far, 8, 128), FAR, 0, 0, tiled=True).reshape(8 * far, 128)
+    def exchange(value, first):
+        parts = value.reshape(far, 8, 128)
+        return swap_parts(parts, FAR, first).reshape(8 * far, 128)
 
     partial = pl.pallas_call(
         factor_kernel,
@@ -395,12 +441,19 @@
         out_shape=rows,
         in_specs=[whole()],
         out_specs=whole(),
-        scratch_shapes=[pltpu.VMEM((256, near * atoms), bf16), pltpu.VMEM((512, near * atoms), bf16)],
+        scratch_shapes=[
+            pltpu.VMEM((256, near * atoms), bf16),
+            pltpu.VMEM((512, near * atoms), bf16),
+            pltpu.VMEM((3, near, atoms), f32),
+            pltpu.VMEM((4, near, atoms), f32),
+        ],
         compiler_params=params,
     )(gathered)
-    spread = exchange(partial)
-
-    place = jnp.stack([lax.axis_index(FAR), lax.axis_index(NEAR)]).astype(jnp.int32)
+    spread = exchange(partial, first_in)
+
+    owner = (lax.axis_index(FAR) + far - first_in) % far
+    share = (lax.axis_index(NEAR) + near - first_near) % near
+    place = jnp.stack([owner, share]).astype(jnp.int32)
     screens = jnp.broadcast_to(screen_len[:, None], (chans, 128))
     coef = pl.pallas_call(
         coef_kernel,
@@ -433,17 +486,32 @@
         out_specs=[whole()] * 2,
         compiler_params=params,
     )(place, spread, coef, step_face, ghosts_1)
-    everywhere = exchange(filtered)
+    everywhere = exchange(filtered, first_out)
     ghosts_2 = lax.ppermute(step_face, DOM, step)
+    early = near * 3 // 4
+    field_scratch = [
+        pltpu.VMEM((256, max(early, near - early) * atoms), bf16),
+        pltpu.VMEM((512, 256), bf16),
+        pltpu.VMEM((3, near, atoms), f32),
+    ]
     field = pl.pallas_call(
         field_kernel,
         name="field",
+        out_shape=jax.ShapeDtypeStruct((early, 4, atoms), f32),
+        in_specs=[whole()] * 2,
+        out_specs=whole(),
+        scratch_shapes=field_scratch,
+        compiler_params=params,
+    )(everywhere, gathered)
+    field = pl.pallas_call(
+        rest_kernel,
+        name="rest",
         out_shape=jax.ShapeDtypeStruct((near, 4, atoms), f32),
-        in_specs=[whole(), whole(), whole(pl.ANY)],
+        in_specs=[whole()] * 3 + [whole(pl.ANY)],
         out_specs=whole(),
-        scratch_shapes=[pltpu.VMEM((256, near * atoms), bf16), pltpu.VMEM((512, 256), bf16)],
-        compiler_params=params,
-    )(everywhere, gathered, ghosts_2)
+        scratch_shapes=field_scratch,
+        compiler_params=params,
+    )(everywhere, gathered, field, ghosts_2)
     base, twice = pl.pallas_call(
         short_kernel,
         name="short",
@@ -453,7 +521,7 @@
         compiler_params=params,
         cost_estimate=pl.CostEstimate(flops=2 * 256 * 1280 * atoms, bytes_accessed=10 * 32 * atoms, transcendentals=1280 * atoms),
     )(counts, positions, features, ghosts_1, ghosts_2, long_weight, short_weight, field)
-    longmsg = lax.all_to_all(field, NEAR, 0, 0, tiled=True).reshape(chans, atoms)
+    longmsg = swap_parts(field, NEAR, first_near).reshape(chans, atoms)
     all_atoms = atoms * lax.axis_size(ALL)
     long_scale = long_gain / math.sqrt(total_vec * all_atoms)
     return pl.pallas_call(

time: 83.5 us -> 76.7 us (0.919)
  waiting for transfers between devices: 12 us -> 2.78 us
  starting transfers between devices: 34.9 us -> 39.9 us
  blocking collectives: 16.7 us -> 13.9 us
    all_to_all x3, starting transfers between devices: 24.1 us -> 31.2 us  [swap_parts(): lax.all_to_all(parts, axis, 0, 0, axis_index_groups=order, tiled=True)]
    all_to_all x3, waiting for transfers between devices: 9.84 us -> 2.78 us  [swap_parts(): lax.all_to_all(parts, axis, 0, 0, axis_index_groups=order, tiled=True)]
    all_to_all x1, blocking collectives: 16.7 us -> 13.9 us  [swap_parts(): lax.all_to_all(parts, axis, 0, 0, axis_index_groups=order, tiled=True)]
    ppermute x1, waiting for transfers between devices: 2.14 us -> 0.01 us  [local(): ghosts_2 = lax.ppermute(step_face, DOM, step)]
    ppermute x1, starting transfers between devices: 7.6 us -> 5.48 us  [local(): ghosts_2 = lax.ppermute(step_face, DOM, step)]
    pallas_call x0 -> x1, Pallas kernels: none -> 1.76 us  [local(): pl.pallas_call(rest_kernel, name='rest', out_shape=jax.ShapeDtypeStruct((...]
    pallas_call x1, Pallas kernels: 4.98 us -> 3.32 us  [local(): pl.pallas_call(field_kernel, name='field', out_shape=jax.ShapeDtypeStruct...]
  transfers between devices with their start and end apart: 5 -> 5, of which waited for: 4 -> 2; matrix products, arithmetic and copies ran while one was open for 0% -> 0% of each run, Pallas kernels for 6% -> 10%
where the time goes in v3:
time: 76.7 us; the launch traced here: 76.1 us
  starting transfers between devices  39.9 us (52%)
  Pallas kernels  17.8 us (23%)
  blocking collectives  13.9 us (18%)
  waiting for transfers between devices  2.78 us (4%)
  local copies, waits for them, and re-layouts  0.86 us (1%)
  between operations  0.82 us (1%)
    all_to_all x3, starting transfers between devices, swap_parts(): lax.all_to_all(parts, axis, 0, 0, axis_index_groups=order, tiled=True)  31.2 us
    all_to_all x1, blocking collectives, swap_parts(): lax.all_to_all(parts, axis, 0, 0, axis_index_groups=order, tiled=True)  13.9 us
    ppermute x1, starting transfers between devices, local(): ghosts_2 = lax.ppermute(step_face, DOM, step)  5.48 us
    pallas_call x1, Pallas kernels, local(): pl.pallas_call(factor_kernel, name='factor', out_shape=rows, in_specs=[wh...  4.39 us
    pallas_call x1, Pallas kernels, local(): pl.pallas_call(field_kernel, name='field', out_shape=jax.ShapeDtypeStruct...  3.32 us
    ppermute x1, starting transfers between devices, local(): ghosts_1 = lax.ppermute(flip_face, DOM, flip)  3.18 us
    pallas_call x1, Pallas kernels, local(): pl.pallas_call(short_kernel, name='short', out_shape=[jax.ShapeDtypeStruc...  3.08 us
    all_to_all x3, waiting for transfers between devices, swap_parts(): lax.all_to_all(parts, axis, 0, 0, axis_index_groups=order, tiled=True)  2.78 us
  transfers between devices with their start and end apart: 5, of which 2 were waited for; matrix products, arithmetic and copies ran while one was open for 0% of the time, Pallas kernels for 10%

profile of v3, /device:TPU:1, one launch (start us, length us, event | category | flops | bytes accessed | tf_op | source)
XLA Modules:
  0.0 76.1 jit_solution(11481385889254222356)
XLA Ops:
  0.7 1.6 %prep.1 = s32[8,4,1024]{2,1,0:T(4,128)} custom-call(s32[1]{0:T(128)S(6)} %copy.9.count_ref.refs_0_, f32[3,1024]{1,0:T(4,128)} %pos_ref.3, bf16[32,1024]{1,0:T(8,128)(2,1)} %feat_ref.3), custom_call_target="tpu_custom_call" | custom-call | tf_op jit(solution)/shard_map/prep/pallas_call | solution.py:418
  2.3 13.9 %all_to_all.20.in_ref = s32[8,4,1024]{2,1,0:T(4,128)S(1)} all-to-all(s32[8,4,1024]{2,1,0:T(4,128)} %prep.1), channel_id=1, replica_groups={{256,288,384,416,0,32,128,160},{257,289,385,417,1,33,129,161},{258,290,..., dimensions={0} | all-to-all | bytes 262144 | tf_op jit(solution)/shard_map/all_to_all | solution.py:403
  16.1 4.4 %factor.1.after_ref = bf16[512,128]{1,0:T(8,128)(2,1)} custom-call(s32[8,4,1024]{2,1,0:T(4,128)S(1)} %all_to_all.20.in_ref), custom_call_target="tpu_custom_call" | custom-call | tf_op jit(solution)/shard_map/factor/pallas_call | solution.py:438
  20.5 12.6 %all-to-all-start.1 = ((bf16[64,8,128]{2,1,0:T(8,128)(2,1)}), bf16[64,8,128]{2,1,0:T(8,128)(2,1)S(1)}, u32[]{:S(2)}, u32[]{:S(2)}) async-start(bf16[64,8,128]{2,1,0:T(8,128)(2,1)} %bitcast.3), calls=%async_computation.1 | async-start | bytes 262144 | tf_op jit(solution)/shard_map/all_to_all | solution.py:403
  33.2 0.0 copy-start
  33.2 0.0 copy-start.1
  33.2 0.1 pad_add_fusion.where_ref
  33.3 0.0 copy-start.2
  33.3 0.0 copy-start.3
  33.3 0.7 copy-done
  34.0 0.0 copy-done.1
  34.0 0.0 copy-done.2
  34.0 0.2 faces.1
  34.2 0.0 copy-start.6
  34.2 3.2 %collective-permute-start = (f32[40,128]{1,0:T(8,128)S(1)}, f32[40,128]{1,0:T(8,128)S(1)}, u32[]{:S(2)}, u32[]{:S(2)}) collective-permute-start(f32[40,128]{1,0:T(8,128)S(1)} %get-tuple-element.11), channel_id=1, source_target_pairs={{0,32},{32,0},{64,96},{96,64},{128,160},{160,128},{192,224},{224,1... | collective-permute-start | bytes 61448 | tf_op jit(solution)/shard_map/ppermute | solution.py:480
  37.4 0.0 copy-done.6
  37.4 0.1 broadcast_in_dim.2.screen_ref
  37.5 0.0 copy-done.3
  37.5 1.4 %coef.1.coef_ref = f32[8,8,128]{2,1,0:T(8,128)S(1)} custom-call(s32[2]{0:T(128)S(1)} %pad_add_fusion.where_ref, s32[3,8192]{1,0:T(4,128)S(1)} %copy-done.3, f32[32,128]{1,0:T(8,128)S(1)} %broadcast_in_dim.2.screen_ref, bf16[512,128]{1,0:T(8,128)(2,1)} %factor.1.after_ref), custom_call_target="tpu_custom_call" | custom-call | flops 268435456 | bytes 65536 | tf_op jit(solution)/shard_map/coef/pallas_call | solution.py:458
  38.9 0.0 collective-permute-done.g1_ref
  38.9 1.1 %all-to-all-done.1 = bf16[64,8,128]{2,1,0:T(8,128)(2,1)S(1)} async-done(((bf16[64,8,128]{2,1,0:T(8,128)(2,1)}), bf16[64,8,128]{2,1,0:T(8,128)(2,1)S(1)}, u32[]{:S(2)}, u32[]{:S(2)}) %all-to-all-start.1) | async-done | bytes 131104 | tf_op jit(solution)/shard_map/all_to_all | solution.py:403
  40.1 1.3 %owner.1 = (bf16[512,128]{1,0:T(8,128)(2,1)}, f32[40,128]{1,0:T(8,128)S(1)}) custom-call(s32[2]{0:T(128)S(1)} %pad_add_fusion.where_ref, bf16[512,128]{1,0:T(8,128)(2,1)S(1)} %bitcast.9, f32[8,8,128]{2,1,0:T(8,128)S(1)} %coef.1.coef_ref, f32[40,128]{1,0:T(8,128)S(1)} %get-tuple-element.12.step_ref, f32[40,128]{1,0:T(8,128)S(1)} %collective-permute-done.g1_ref), custom_call_target="tpu_custom_call" | custom-call | tf_op jit(solution)/shard_map/owner/pallas_call | solution.py:481
  41.4 11.0 %all-to-all-start.2 = ((bf16[64,8,128]{2,1,0:T(8,128)(2,1)}), bf16[64,8,128]{2,1,0:T(8,128)(2,1)S(1)}, u32[]{:S(2)}, u32[]{:S(2)}) async-start(bf16[64,8,128]{2,1,0:T(8,128)(2,1)} %bitcast.5), calls=%async_computation.2 | async-start | bytes 262144 | tf_op jit(solution)/shard_map/all_to_all | solution.py:403
  52.3 5.5 %collective-permute-start.1 = (f32[40,128]{1,0:T(8,128)S(1)}, f32[40,128]{1,0:T(8,128)S(1)}, u32[]{:S(2)}, u32[]{:S(2)}) collective-permute-start(f32[40,128]{1,0:T(8,128)S(1)} %get-tuple-element.13), channel_id=1, source_target_pairs={{0,480},{32,64},{64,32},{96,128},{128,96},{160,192},{192,160},{224... | collective-permute-start | bytes 61448 | tf_op jit(solution)/shard_map/ppermute | solution.py:490
  57.8 1.6 %all-to-all-done.2 = bf16[64,8,128]{2,1,0:T(8,128)(2,1)S(1)} async-done(((bf16[64,8,128]{2,1,0:T(8,128)(2,1)}), bf16[64,8,128]{2,1,0:T(8,128)(2,1)S(1)}, u32[]{:S(2)}, u32[]{:S(2)}) %all-to-all-start.2) | async-done | bytes 131104 | tf_op jit(solution)/shard_map/all_to_all | solution.py:403
  59.5 3.3 %field.1.part_ref = f32[6,4,1024]{2,1,0:T(4,128)S(1)} custom-call(bf16[512,128]{1,0:T(8,128)(2,1)S(1)} %bitcast.7, s32[8,4,1024]{2,1,0:T(4,128)S(1)} %all_to_all.20.in_ref), custom_call_target="tpu_custom_call" | custom-call | tf_op jit(solution)/shard_map/field/pallas_call | solution.py:497
  62.8 0.0 collective-permute-done.1.g2_ref
  62.8 1.8 %rest.1.after_ref = f32[8,4,1024]{2,1,0:T(4,128)} custom-call(bf16[512,128]{1,0:T(8,128)(2,1)S(1)} %bitcast.8, s32[8,4,1024]{2,1,0:T(4,128)S(1)} %all_to_all.20.in_ref, f32[6,4,1024]{2,1,0:T(4,128)S(1)} %field.1.part_ref, f32[40,128]{1,0:T(8,128)S(1)} %collective-permute-done.1.g2_ref), custom_call_target="tpu_custom_call" | custom-call | tf_op jit(solution)/shard_map/rest/pallas_call | solution.py:506
  64.6 0.0 copy-start.4
  64.6 0.0 copy-start.5
  64.6 7.6 %all-to-all-start.3 = ((f32[8,4,1024]{2,1,0:T(4,128)}), f32[8,4,1024]{2,1,0:T(4,128)S(1)}, u32[]{:S(2)}, u32[]{:S(2)}) async-start(f32[8,4,1024]{2,1,0:T(4,128)} %rest.1.after_ref), calls=%async_computation.3 | async-start | bytes 262144 | tf_op jit(solution)/shard_map/all_to_all | solution.py:403
  72.2 0.0 copy-done.4
  72.2 0.0 copy-done.5
  72.2 3.1 %short.1 = (f32[32,1024]{1,0:T(8,128)S(1)}, bf16[32,64]{1,0:T(8,128)(2,1)S(1)}) custom-call(s32[1]{0:T(128)S(6)} %copy.9.count_ref.refs_0_, f32[3,1024]{1,0:T(4,128)S(1)} %copy-done.1, bf16[32,1024]{1,0:T(8,128)(2,1)S(1)} %copy-done, f32[40,128]{1,0:T(8,128)S(1)} %collective-permute-done.g1_ref, f32[40,128]{1,0:T(8,128)S(1)} %collective-permute-done.1.g2_ref, ...), custom_call_target="tpu_custom_call" | custom-call | flops 671088640 | bytes 327680 | tf_op jit(solution)/shard_map/short/pallas_call | solution.py:515
  75.3 0.0 all-to-all-done.3
  75.3 0.8 %final.1 = bf16[32,1024]{1,0:T(8,128)(2,1)} custom-call(s32[1]{0:T(128)S(6)} %copy.9.count_ref.refs_0_, f32[32,1024]{1,0:T(8,128)S(1)} %get-tuple-element.15.refs_1_, f32[32,1024]{1,0:T(8,128)S(1)} %reshape.24.refs_2_, bf16[32,64]{1,0:T(8,128)(2,1)S(1)} %get-tuple-element.16.refs_3_), custom_call_target="tpu_custom_call" | custom-call | tf_op jit(solution)/shard_map/final/pallas_call | solution.py:527
  (1 shorter events, 0.0 us)
Async XLA Ops:
  20.5 19.5 %all-to-all-start.1 = ((bf16[64,8,128]{2,1,0:T(8,128)(2,1)}), bf16[64,8,128]{2,1,0:T(8,128)(2,1)S(1)}, u32[]{:S(2)}, u32[]{:S(2)}) async-start(bf16[64,8,128]{2,1,0:T(8,128)(2,1)} %bitcast.3), calls=%async_computation.1 | async-start | bytes 262144 | tf_op jit(solution)/shard_map/all_to_all | solution.py:403
  33.2 0.8 %copy-start = (bf16[32,1024]{1,0:T(8,128)(2,1)S(1)}, bf16[32,1024]{1,0:T(8,128)(2,1)}, u32[]{:S(2)}) copy-start(bf16[32,1024]{1,0:T(8,128)(2,1)} %feat_ref.3) | copy-start | bytes 196612
  33.2 0.8 %copy-start.1 = (f32[3,1024]{1,0:T(4,128)S(1)}, f32[3,1024]{1,0:T(4,128)}, u32[]{:S(2)}) copy-start(f32[3,1024]{1,0:T(4,128)} %pos_ref.3) | copy-start | bytes 36868
  33.3 0.7 copy-start.2
  33.3 4.2 %copy-start.3 = (s32[3,8192]{1,0:T(4,128)S(1)}, s32[3,8192]{1,0:T(4,128)}, u32[]{:S(2)}) copy-start(s32[3,8192]{1,0:T(4,128)} %kvec_ref.1) | copy-start | bytes 294916
  34.2 3.2 %copy-start.6 = (f32[32]{0:T(128)S(1)}, f32[32]{0:T(128)}, u32[]{:S(2)}) copy-start(f32[32]{0:T(128)} %param.13) | copy-start | bytes 388
  34.2 4.7 %collective-permute-start = (f32[40,128]{1,0:T(8,128)S(1)}, f32[40,128]{1,0:T(8,128)S(1)}, u32[]{:S(2)}, u32[]{:S(2)}) collective-permute-start(f32[40,128]{1,0:T(8,128)S(1)} %get-tuple-element.11), channel_id=1, source_target_pairs={{0,32},{32,0},{64,96},{96,64},{128,160},{160,128},{192,224},{224,1... | collective-permute-start | bytes 61448 | tf_op jit(solution)/shard_map/ppermute | solution.py:480
  41.4 18.1 %all-to-all-start.2 = ((bf16[64,8,128]{2,1,0:T(8,128)(2,1)}), bf16[64,8,128]{2,1,0:T(8,128)(2,1)S(1)}, u32[]{:S(2)}, u32[]{:S(2)}) async-start(bf16[64,8,128]{2,1,0:T(8,128)(2,1)} %bitcast.5), calls=%async_computation.2 | async-start | bytes 262144 | tf_op jit(solution)/shard_map/all_to_all | solution.py:403
  52.3 10.4 %collective-permute-start.1 = (f32[40,128]{1,0:T(8,128)S(1)}, f32[40,128]{1,0:T(8,128)S(1)}, u32[]{:S(2)}, u32[]{:S(2)}) collective-permute-start(f32[40,128]{1,0:T(8,128)S(1)} %get-tuple-element.13), channel_id=1, source_target_pairs={{0,480},{32,64},{64,32},{96,128},{128,96},{160,192},{192,160},{224... | collective-permute-start | bytes 61448 | tf_op jit(solution)/shard_map/ppermute | solution.py:490
  64.6 7.6 %copy-start.4 = (bf16[32,32]{1,0:T(8,128)(2,1)S(1)}, bf16[32,32]{1,0:T(8,128)(2,1)}, u32[]{:S(2)}) copy-start(bf16[32,32]{1,0:T(8,128)(2,1)} %lw_ref.1) | copy-start | bytes 6148
  64.6 7.6 %copy-start.5 = (bf16[32,32]{1,0:T(8,128)(2,1)S(1)}, bf16[32,32]{1,0:T(8,128)(2,1)}, u32[]{:S(2)}) copy-start(bf16[32,32]{1,0:T(8,128)(2,1)} %sw_ref.1) | copy-start | bytes 6148
  64.6 10.7 %all-to-all-start.3 = ((f32[8,4,1024]{2,1,0:T(4,128)}), f32[8,4,1024]{2,1,0:T(4,128)S(1)}, u32[]{:S(2)}, u32[]{:S(2)}) async-start(f32[8,4,1024]{2,1,0:T(4,128)} %rest.1.after_ref), calls=%async_computation.3 | async-start | bytes 262144 | tf_op jit(solution)/shard_map/all_to_all | solution.py:403

commit v4 on v3

--- a/solution.py
+++ b/solution.py
@@ -332,7 +332,8 @@
         out_ref[k] = jnp.concatenate(lines, axis=0)
 
 
-def field_kernel(filt_ref, in_ref, out_ref, e_ref, g_ref, turns_ref):
+def field_kernel(filt_ref, in_ref, own_ref, out_ref, e_ref, g_ref, turns_ref):
+    del own_ref
     field_blocks(0, filt_ref, in_ref, out_ref, e_ref, g_ref, turns_ref)
 
 
@@ -358,25 +359,28 @@
     return jnp.exp2(-(dx * dx + dy * dy + dz * dz)).astype(bf16)
 
 
-def short_kernel(
-    count_ref, pos_ref, feat_ref, g1_ref, g2_ref, lw_ref, sw_ref, after_ref, base_ref, twice_ref
-):
+def own_kernel(count_ref, pos_ref, feat_ref, after_ref, out_ref):
     del after_ref
     atoms = pos_ref.shape[1]
-    feat = feat_ref[...].astype(f32)
-    masked = (feat * valid_row(count_ref, atoms)).astype(bf16)
+    masked = (feat_ref[...].astype(f32) * valid_row(count_ref, atoms)).astype(bf16)
     rows = pos_ref[...] * shrink
     rows8 = jnp.concatenate([rows, jnp.zeros((5, atoms), f32)], axis=0)
-    ghost = jnp.concatenate([g1_ref[...], g2_ref[...]], axis=1)
-    near_by = pairs(jnp.transpose(ghost[32:40] * shrink), rows, True)
-    short = jnp.dot(ghost[0:32].astype(bf16), near_by, preferred_element_type=f32)
     step = 256
+    total = None
     for n in range(atoms // step):
         at = slice(n * step, (n + 1) * step)
-        own = pairs(jnp.transpose(rows8[:, at]), rows, False)
-        short = short + jnp.dot(masked[:, at], own, preferred_element_type=f32)
+        term = jnp.dot(masked[:, at], pairs(jnp.transpose(rows8[:, at]), rows, False), preferred_element_type=f32)
+        total = term if total is None else total + term
+    out_ref[...] = total
+
+
+def short_kernel(pos_ref, feat_ref, g1_ref, g2_ref, own_ref, lw_ref, sw_ref, after_ref, base_ref, twice_ref):
+    del after_ref
+    ghost = jnp.concatenate([g1_ref[...], g2_ref[...]], axis=1)
+    near_by = pairs(jnp.transpose(ghost[32:40] * shrink), pos_ref[...] * shrink, True)
+    short = own_ref[...] + jnp.dot(ghost[0:32].astype(bf16), near_by, preferred_element_type=f32)
     mixed = jnp.dot(stacked(sw_ref[...]), split(short), preferred_element_type=f32)
-    base_ref[...] = feat + short_gain * mixed
+    base_ref[...] = feat_ref[...].astype(f32) + short_gain * mixed
     twice_ref[...] = stacked(lw_ref[...])
 
 
@@ -488,7 +492,15 @@
     )(place, spread, coef, step_face, ghosts_1)
     everywhere = exchange(filtered, first_out)
     ghosts_2 = lax.ppermute(step_face, DOM, step)
-    early = near * 3 // 4
+    own = pl.pallas_call(
+        own_kernel,
+        name="own",
+        out_shape=jax.ShapeDtypeStruct((chans, atoms), f32),
+        in_specs=[whole(pltpu.SMEM), whole(), whole(), whole(pl.ANY)],
+        out_specs=whole(),
+        compiler_params=params,
+    )(counts, positions, features, filtered)
+    early = near * 7 // 8
     field_scratch = [
         pltpu.VMEM((256, max(early, near - early) * atoms), bf16),
         pltpu.VMEM((512, 256), bf16),
@@ -498,11 +510,11 @@
         field_kernel,
         name="field",
         out_shape=jax.ShapeDtypeStruct((early, 4, atoms), f32),
-        in_specs=[whole()] * 2,
+        in_specs=[whole()] * 2 + [whole(pl.ANY)],
         out_specs=whole(),
         scratch_shapes=field_scratch,
         compiler_params=params,
-    )(everywhere, gathered)
+    )(everywhere, gathered, own)
     field = pl.pallas_call(
         rest_kernel,
         name="rest",
@@ -516,11 +528,11 @@
         short_kernel,
         name="short",
         out_shape=[jax.ShapeDtypeStruct((chans, atoms), f32), jax.ShapeDtypeStruct((chans, 2 * chans), bf16)],
-        in_specs=[whole(pltpu.SMEM)] + [whole()] * 6 + [whole(pl.ANY)],
+        in_specs=[whole()] * 7 + [whole(pl.ANY)],
         out_specs=[whole()] * 2,
         compiler_params=params,
-        cost_estimate=pl.CostEstimate(flops=2 * 256 * 1280 * atoms, bytes_accessed=10 * 32 * atoms, transcendentals=1280 * atoms),
-    )(counts, positions, features, ghosts_1, ghosts_2, long_weight, short_weight, field)
+        cost_estimate=pl.CostEstimate(flops=2 * 256 * 256 * atoms, bytes_accessed=10 * 32 * atoms, transcendentals=256 * atoms),
+    )(positions, features, ghosts_1, ghosts_2, own, long_weight, short_weight, field)
     longmsg = swap_parts(field, NEAR, first_near).reshape(chans, atoms)
     all_atoms = atoms * lax.axis_size(ALL)
     long_scale = long_gain / math.sqrt(total_vec * all_atoms)

time: 76.7 us -> 76.1 us (level)
  starting transfers between devices: 39.9 us -> 39.1 us
    pallas_call x0 -> x1, Pallas kernels: none -> 2.35 us  [local(): pl.pallas_call(own_kernel, name='own', out_shape=jax.ShapeDtypeStruct((ch...]
    pallas_call x1, Pallas kernels: 3.08 us -> 1 us  [local(): pl.pallas_call(short_kernel, name='short', out_shape=[jax.ShapeDtypeStruc...]
    all_to_all x3, starting transfers between devices: 31.2 us -> 30.3 us  [swap_parts(): lax.all_to_all(parts, axis, 0, 0, axis_index_groups=order, tiled=True)]
  transfers between devices with their start and end apart: 5 -> 5, of which waited for: 2 -> 2; matrix products, arithmetic and copies ran while one was open for 0% -> 0% of each run, Pallas kernels for 10% -> 12%
where the time goes in v4:
time: 76.1 us; the launch traced here: 75.6 us
  starting transfers between devices  39.1 us (51%)
  Pallas kernels  18.1 us (24%)
  blocking collectives  13.9 us (18%)
  waiting for transfers between devices  2.69 us (4%)
  local copies, waits for them, and re-layouts  0.86 us (1%)
  between operations  0.82 us (1%)
    all_to_all x3, starting transfers between devices, swap_parts(): lax.all_to_all(parts, axis, 0, 0, axis_index_groups=order, tiled=True)  30.3 us
    all_to_all x1, blocking collectives, swap_parts(): lax.all_to_all(parts, axis, 0, 0, axis_index_groups=order, tiled=True)  13.9 us
    ppermute x1, starting transfers between devices, local(): ghosts_2 = lax.ppermute(step_face, DOM, step)  5.66 us
    pallas_call x1, Pallas kernels, local(): pl.pallas_call(factor_kernel, name='factor', out_shape=rows, in_specs=[wh...  4.39 us
    pallas_call x1, Pallas kernels, local(): pl.pallas_call(field_kernel, name='field', out_shape=jax.ShapeDtypeStruct...  3.87 us
    ppermute x1, starting transfers between devices, local(): ghosts_1 = lax.ppermute(flip_face, DOM, flip)  3.18 us
    all_to_all x3, waiting for transfers between devices, swap_parts(): lax.all_to_all(parts, axis, 0, 0, axis_index_groups=order, tiled=True)  2.68 us
    pallas_call x1, Pallas kernels, local(): pl.pallas_call(own_kernel, name='own', out_shape=jax.ShapeDtypeStruct((ch...  2.35 us
  transfers between devices with their start and end apart: 5, of which 2 were waited for; matrix products, arithmetic and copies ran while one was open for 0% of the time, Pallas kernels for 12%

profile of v4, /device:TPU:1, one launch (start us, length us, event | category | flops | bytes accessed | tf_op | source)
XLA Modules:
  0.0 75.6 jit_solution(9144013905758267291)
XLA Ops:
  0.7 1.6 %prep.1 = s32[8,4,1024]{2,1,0:T(4,128)} custom-call(s32[1]{0:T(128)S(6)} %copy.9.count_ref.refs_0_, f32[3,1024]{1,0:T(4,128)} %pos_ref.5, bf16[32,1024]{1,0:T(8,128)(2,1)} %feat_ref.5), custom_call_target="tpu_custom_call" | custom-call | tf_op jit(solution)/shard_map/prep/pallas_call | solution.py:422
  2.3 13.9 %all_to_all.20.in_ref = s32[8,4,1024]{2,1,0:T(4,128)S(1)} all-to-all(s32[8,4,1024]{2,1,0:T(4,128)} %prep.1), channel_id=1, replica_groups={{256,288,384,416,0,32,128,160},{257,289,385,417,1,33,129,161},{258,290,..., dimensions={0} | all-to-all | bytes 262144 | tf_op jit(solution)/shard_map/all_to_all | solution.py:407
  16.1 4.4 %factor.1.after_ref = bf16[512,128]{1,0:T(8,128)(2,1)} custom-call(s32[8,4,1024]{2,1,0:T(4,128)S(1)} %all_to_all.20.in_ref), custom_call_target="tpu_custom_call" | custom-call | tf_op jit(solution)/shard_map/factor/pallas_call | solution.py:442
  20.5 12.6 %all-to-all-start.1 = ((bf16[64,8,128]{2,1,0:T(8,128)(2,1)}), bf16[64,8,128]{2,1,0:T(8,128)(2,1)S(1)}, u32[]{:S(2)}, u32[]{:S(2)}) async-start(bf16[64,8,128]{2,1,0:T(8,128)(2,1)} %bitcast.3), calls=%async_computation.1 | async-start | bytes 262144 | tf_op jit(solution)/shard_map/all_to_all | solution.py:407
  33.2 0.0 copy-start
  33.2 0.0 copy-start.1
  33.2 0.1 pad_add_fusion.where_ref
  33.3 0.0 copy-start.2
  33.3 0.0 copy-start.3
  33.3 0.7 copy-done
  34.0 0.0 copy-done.1
  34.0 0.0 copy-done.2
  34.0 0.2 faces.1
  34.2 0.0 copy-start.6
  34.2 3.2 %collective-permute-start = (f32[40,128]{1,0:T(8,128)S(1)}, f32[40,128]{1,0:T(8,128)S(1)}, u32[]{:S(2)}, u32[]{:S(2)}) collective-permute-start(f32[40,128]{1,0:T(8,128)S(1)} %get-tuple-element.11), channel_id=1, source_target_pairs={{0,32},{32,0},{64,96},{96,64},{128,160},{160,128},{192,224},{224,1... | collective-permute-start | bytes 61448 | tf_op jit(solution)/shard_map/ppermute | solution.py:484
  37.4 0.0 copy-done.6
  37.4 0.1 broadcast_in_dim.2.screen_ref
  37.5 0.0 copy-done.3
  37.5 1.4 %coef.1.coef_ref = f32[8,8,128]{2,1,0:T(8,128)S(1)} custom-call(s32[2]{0:T(128)S(1)} %pad_add_fusion.where_ref, s32[3,8192]{1,0:T(4,128)S(1)} %copy-done.3, f32[32,128]{1,0:T(8,128)S(1)} %broadcast_in_dim.2.screen_ref, bf16[512,128]{1,0:T(8,128)(2,1)} %factor.1.after_ref), custom_call_target="tpu_custom_call" | custom-call | flops 268435456 | bytes 65536 | tf_op jit(solution)/shard_map/coef/pallas_call | solution.py:462
  38.9 0.0 collective-permute-done.g1_ref
  38.9 1.1 %all-to-all-done.1 = bf16[64,8,128]{2,1,0:T(8,128)(2,1)S(1)} async-done(((bf16[64,8,128]{2,1,0:T(8,128)(2,1)}), bf16[64,8,128]{2,1,0:T(8,128)(2,1)S(1)}, u32[]{:S(2)}, u32[]{:S(2)}) %all-to-all-start.1) | async-done | bytes 131104 | tf_op jit(solution)/shard_map/all_to_all | solution.py:407
  40.1 1.3 %owner.1 = (bf16[512,128]{1,0:T(8,128)(2,1)}, f32[40,128]{1,0:T(8,128)S(1)}) custom-call(s32[2]{0:T(128)S(1)} %pad_add_fusion.where_ref, bf16[512,128]{1,0:T(8,128)(2,1)S(1)} %bitcast.9, f32[8,8,128]{2,1,0:T(8,128)S(1)} %coef.1.coef_ref, f32[40,128]{1,0:T(8,128)S(1)} %get-tuple-element.12.step_ref, f32[40,128]{1,0:T(8,128)S(1)} %collective-permute-done.g1_ref), custom_call_target="tpu_custom_call" | custom-call | tf_op jit(solution)/shard_map/owner/pallas_call | solution.py:485
  41.4 11.0 %all-to-all-start.2 = ((bf16[64,8,128]{2,1,0:T(8,128)(2,1)}), bf16[64,8,128]{2,1,0:T(8,128)(2,1)S(1)}, u32[]{:S(2)}, u32[]{:S(2)}) async-start(bf16[64,8,128]{2,1,0:T(8,128)(2,1)} %bitcast.5), calls=%async_computation.2 | async-start | bytes 262144 | tf_op jit(solution)/shard_map/all_to_all | solution.py:407
  52.3 5.7 %collective-permute-start.1 = (f32[40,128]{1,0:T(8,128)S(1)}, f32[40,128]{1,0:T(8,128)S(1)}, u32[]{:S(2)}, u32[]{:S(2)}) collective-permute-start(f32[40,128]{1,0:T(8,128)S(1)} %get-tuple-element.13), channel_id=1, source_target_pairs={{0,480},{32,64},{64,32},{96,128},{128,96},{160,192},{192,160},{224... | collective-permute-start | bytes 61448 | tf_op jit(solution)/shard_map/ppermute | solution.py:494
  58.0 2.3 %own.1.own_ref = f32[32,1024]{1,0:T(8,128)S(1)} custom-call(s32[1]{0:T(128)S(6)} %copy.9.count_ref.refs_0_, f32[3,1024]{1,0:T(4,128)S(1)} %copy-done.1, bf16[32,1024]{1,0:T(8,128)(2,1)S(1)} %copy-done, bf16[512,128]{1,0:T(8,128)(2,1)} %get-tuple-element.14.after_ref), custom_call_target="tpu_custom_call" | custom-call | tf_op jit(solution)/shard_map/own/pallas_call | solution.py:495
  60.4 0.0 all-to-all-done.2
  60.4 3.9 %field.1.part_ref = f32[7,4,1024]{2,1,0:T(4,128)S(1)} custom-call(bf16[512,128]{1,0:T(8,128)(2,1)S(1)} %bitcast.7, s32[8,4,1024]{2,1,0:T(4,128)S(1)} %all_to_all.20.in_ref, f32[32,1024]{1,0:T(8,128)S(1)} %own.1.own_ref), custom_call_target="tpu_custom_call" | custom-call | tf_op jit(solution)/shard_map/field/pallas_call | solution.py:509
  64.3 0.0 collective-permute-done.1.g2_ref
  64.3 1.2 %rest.1.after_ref = f32[8,4,1024]{2,1,0:T(4,128)} custom-call(bf16[512,128]{1,0:T(8,128)(2,1)S(1)} %bitcast.8, s32[8,4,1024]{2,1,0:T(4,128)S(1)} %all_to_all.20.in_ref, f32[7,4,1024]{2,1,0:T(4,128)S(1)} %field.1.part_ref, f32[40,128]{1,0:T(8,128)S(1)} %collective-permute-done.1.g2_ref), custom_call_target="tpu_custom_call" | custom-call | tf_op jit(solution)/shard_map/rest/pallas_call | solution.py:518
  65.5 0.0 copy-start.4
  65.5 0.0 copy-start.5
  65.5 6.7 %all-to-all-start.3 = ((f32[8,4,1024]{2,1,0:T(4,128)}), f32[8,4,1024]{2,1,0:T(4,128)S(1)}, u32[]{:S(2)}, u32[]{:S(2)}) async-start(f32[8,4,1024]{2,1,0:T(4,128)} %rest.1.after_ref), calls=%async_computation.3 | async-start | bytes 262144 | tf_op jit(solution)/shard_map/all_to_all | solution.py:407
  72.2 0.0 copy-done.4
  72.2 0.0 copy-done.5
  72.2 1.0 %short.1 = (f32[32,1024]{1,0:T(8,128)S(1)}, bf16[32,64]{1,0:T(8,128)(2,1)S(1)}) custom-call(f32[3,1024]{1,0:T(4,128)S(1)} %copy-done.1, bf16[32,1024]{1,0:T(8,128)(2,1)S(1)} %copy-done, f32[40,128]{1,0:T(8,128)S(1)} %collective-permute-done.g1_ref, f32[40,128]{1,0:T(8,128)S(1)} %collective-permute-done.1.g2_ref, f32[32,1024]{1,0:T(8,128)S(1)} %own.1.own_ref, ...), custom_call_target="tpu_custom_call" | custom-call | flops 134217728 | bytes 327680 | tf_op jit(solution)/shard_map/short/pallas_call | solution.py:527
  73.2 1.5 %all-to-all-done.3 = f32[8,4,1024]{2,1,0:T(4,128)S(1)} async-done(((f32[8,4,1024]{2,1,0:T(4,128)}), f32[8,4,1024]{2,1,0:T(4,128)S(1)}, u32[]{:S(2)}, u32[]{:S(2)}) %all-to-all-start.3) | async-done | bytes 131104 | tf_op jit(solution)/shard_map/all_to_all | solution.py:407
  74.8 0.8 %final.1 = bf16[32,1024]{1,0:T(8,128)(2,1)} custom-call(s32[1]{0:T(128)S(6)} %copy.9.count_ref.refs_0_, f32[32,1024]{1,0:T(8,128)S(1)} %get-tuple-element.15.refs_1_, f32[32,1024]{1,0:T(8,128)S(1)} %reshape.24.refs_2_, bf16[32,64]{1,0:T(8,128)(2,1)S(1)} %get-tuple-element.16.refs_3_), custom_call_target="tpu_custom_call" | custom-call | tf_op jit(solution)/shard_map/final/pallas_call | solution.py:539
  (1 shorter events, 0.0 us)
Async XLA Ops:
  20.5 19.5 %all-to-all-start.1 = ((bf16[64,8,128]{2,1,0:T(8,128)(2,1)}), bf16[64,8,128]{2,1,0:T(8,128)(2,1)S(1)}, u32[]{:S(2)}, u32[]{:S(2)}) async-start(bf16[64,8,128]{2,1,0:T(8,128)(2,1)} %bitcast.3), calls=%async_computation.1 | async-start | bytes 262144 | tf_op jit(solution)/shard_map/all_to_all | solution.py:407
  33.2 0.8 %copy-start = (bf16[32,1024]{1,0:T(8,128)(2,1)S(1)}, bf16[32,1024]{1,0:T(8,128)(2,1)}, u32[]{:S(2)}) copy-start(bf16[32,1024]{1,0:T(8,128)(2,1)} %feat_ref.5) | copy-start | bytes 196612
  33.2 0.8 %copy-start.1 = (f32[3,1024]{1,0:T(4,128)S(1)}, f32[3,1024]{1,0:T(4,128)}, u32[]{:S(2)}) copy-start(f32[3,1024]{1,0:T(4,128)} %pos_ref.5) | copy-start | bytes 36868
  33.3 0.7 copy-start.2
  33.3 4.2 %copy-start.3 = (s32[3,8192]{1,0:T(4,128)S(1)}, s32[3,8192]{1,0:T(4,128)}, u32[]{:S(2)}) copy-start(s32[3,8192]{1,0:T(4,128)} %kvec_ref.1) | copy-start | bytes 294916
  34.2 3.2 %copy-start.6 = (f32[32]{0:T(128)S(1)}, f32[32]{0:T(128)}, u32[]{:S(2)}) copy-start(f32[32]{0:T(128)} %param.13) | copy-start | bytes 388
  34.2 4.7 %collective-permute-start = (f32[40,128]{1,0:T(8,128)S(1)}, f32[40,128]{1,0:T(8,128)S(1)}, u32[]{:S(2)}, u32[]{:S(2)}) collective-permute-start(f32[40,128]{1,0:T(8,128)S(1)} %get-tuple-element.11), channel_id=1, source_target_pairs={{0,32},{32,0},{64,96},{96,64},{128,160},{160,128},{192,224},{224,1... | collective-permute-start | bytes 61448 | tf_op jit(solution)/shard_map/ppermute | solution.py:484
  41.4 19.0 %all-to-all-start.2 = ((bf16[64,8,128]{2,1,0:T(8,128)(2,1)}), bf16[64,8,128]{2,1,0:T(8,128)(2,1)S(1)}, u32[]{:S(2)}, u32[]{:S(2)}) async-start(bf16[64,8,128]{2,1,0:T(8,128)(2,1)} %bitcast.5), calls=%async_computation.2 | async-start | bytes 262144 | tf_op jit(solution)/shard_map/all_to_all | solution.py:407
  52.3 11.9 %collective-permute-start.1 = (f32[40,128]{1,0:T(8,128)S(1)}, f32[40,128]{1,0:T(8,128)S(1)}, u32[]{:S(2)}, u32[]{:S(2)}) collective-permute-start(f32[40,128]{1,0:T(8,128)S(1)} %get-tuple-element.13), channel_id=1, source_target_pairs={{0,480},{32,64},{64,32},{96,128},{128,96},{160,192},{192,160},{224... | collective-permute-start | bytes 61448 | tf_op jit(solution)/shard_map/ppermute | solution.py:494
  65.5 6.7 %copy-start.4 = (bf16[32,32]{1,0:T(8,128)(2,1)S(1)}, bf16[32,32]{1,0:T(8,128)(2,1)}, u32[]{:S(2)}) copy-start(bf16[32,32]{1,0:T(8,128)(2,1)} %lw_ref.1) | copy-start | bytes 6148
  65.5 6.7 %copy-start.5 = (bf16[32,32]{1,0:T(8,128)(2,1)S(1)}, bf16[32,32]{1,0:T(8,128)(2,1)}, u32[]{:S(2)}) copy-start(bf16[32,32]{1,0:T(8,128)(2,1)} %sw_ref.1) | copy-start | bytes 6148
  65.5 9.2 %all-to-all-start.3 = ((f32[8,4,1024]{2,1,0:T(4,128)}), f32[8,4,1024]{2,1,0:T(4,128)S(1)}, u32[]{:S(2)}, u32[]{:S(2)}) async-start(f32[8,4,1024]{2,1,0:T(4,128)} %rest.1.after_ref), calls=%async_computation.3 | async-start | bytes 262144 | tf_op jit(solution)/shard_map/all_to_all | solution.py:407

commit v5 on v4

--- a/solution.py
+++ b/solution.py
@@ -15,7 +15,7 @@
 feature_top = 6.0
 feature_steps = 32767.0
 first_in = 59
-first_out = 59
+first_out = 63
 first_near = 4
 vmem_limit = 48 * 1024 * 1024
 

time: 76.1 us -> 75.7 us (level)
  no operation moved by 1% of the time
where the time goes in v5:
time: 75.7 us; the launch traced here: 75.2 us
  starting transfers between devices  38.8 us (51%)
  Pallas kernels  18.1 us (24%)
  blocking collectives  13.9 us (18%)
  waiting for transfers between devices  2.69 us (4%)
  local copies, waits for them, and re-layouts  0.86 us (1%)
  between operations  0.82 us (1%)
    all_to_all x3, starting transfers between devices, swap_parts(): lax.all_to_all(parts, axis, 0, 0, axis_index_groups=order, tiled=True)  29.9 us
    all_to_all x1, blocking collectives, swap_parts(): lax.all_to_all(parts, axis, 0, 0, axis_index_groups=order, tiled=True)  13.9 us
    ppermute x1, starting transfers between devices, local(): ghosts_2 = lax.ppermute(step_face, DOM, step)  5.66 us
    pallas_call x1, Pallas kernels, local(): pl.pallas_call(factor_kernel, name='factor', out_shape=rows, in_specs=[wh...  4.39 us
    pallas_call x1, Pallas kernels, local(): pl.pallas_call(field_kernel, name='field', out_shape=jax.ShapeDtypeStruct...  3.88 us
    ppermute x1, starting transfers between devices, local(): ghosts_1 = lax.ppermute(flip_face, DOM, flip)  3.18 us
    all_to_all x3, waiting for transfers between devices, swap_parts(): lax.all_to_all(parts, axis, 0, 0, axis_index_groups=order, tiled=True)  2.68 us
    pallas_call x1, Pallas kernels, local(): pl.pallas_call(own_kernel, name='own', out_shape=jax.ShapeDtypeStruct((ch...  2.35 us
  transfers between devices with their start and end apart: 5, of which 2 were waited for; matrix products, arithmetic and copies ran while one was open for 0% of the time, Pallas kernels for 12%

profile of v5, /device:TPU:1, one launch (start us, length us, event | category | flops | bytes accessed | tf_op | source)
XLA Modules:
  0.0 75.2 jit_solution(11877354953585395079)
XLA Ops:
  0.7 1.6 %prep.1 = s32[8,4,1024]{2,1,0:T(4,128)} custom-call(s32[1]{0:T(128)S(6)} %copy.9.count_ref.refs_0_, f32[3,1024]{1,0:T(4,128)} %pos_ref.5, bf16[32,1024]{1,0:T(8,128)(2,1)} %feat_ref.5), custom_call_target="tpu_custom_call" | custom-call | tf_op jit(solution)/shard_map/prep/pallas_call | solution.py:422
  2.3 13.9 %all_to_all.20.in_ref = s32[8,4,1024]{2,1,0:T(4,128)S(1)} all-to-all(s32[8,4,1024]{2,1,0:T(4,128)} %prep.1), channel_id=1, replica_groups={{256,288,384,416,0,32,128,160},{257,289,385,417,1,33,129,161},{258,290,..., dimensions={0} | all-to-all | bytes 262144 | tf_op jit(solution)/shard_map/all_to_all | solution.py:407
  16.1 4.4 %factor.1.after_ref = bf16[512,128]{1,0:T(8,128)(2,1)} custom-call(s32[8,4,1024]{2,1,0:T(4,128)S(1)} %all_to_all.20.in_ref), custom_call_target="tpu_custom_call" | custom-call | tf_op jit(solution)/shard_map/factor/pallas_call | solution.py:442
  20.5 12.6 %all-to-all-start.1 = ((bf16[64,8,128]{2,1,0:T(8,128)(2,1)}), bf16[64,8,128]{2,1,0:T(8,128)(2,1)S(1)}, u32[]{:S(2)}, u32[]{:S(2)}) async-start(bf16[64,8,128]{2,1,0:T(8,128)(2,1)} %bitcast.3), calls=%async_computation.1 | async-start | bytes 262144 | tf_op jit(solution)/shard_map/all_to_all | solution.py:407
  33.2 0.0 copy-start
  33.2 0.0 copy-start.1
  33.2 0.1 pad_add_fusion.where_ref
  33.3 0.0 copy-start.2
  33.3 0.0 copy-start.3
  33.3 0.7 copy-done
  34.0 0.0 copy-done.1
  34.0 0.0 copy-done.2
  34.0 0.2 faces.1
  34.2 0.0 copy-start.6
  34.2 3.2 %collective-permute-start = (f32[40,128]{1,0:T(8,128)S(1)}, f32[40,128]{1,0:T(8,128)S(1)}, u32[]{:S(2)}, u32[]{:S(2)}) collective-permute-start(f32[40,128]{1,0:T(8,128)S(1)} %get-tuple-element.11), channel_id=1, source_target_pairs={{0,32},{32,0},{64,96},{96,64},{128,160},{160,128},{192,224},{224,1... | collective-permute-start | bytes 61448 | tf_op jit(solution)/shard_map/ppermute | solution.py:484
  37.4 0.0 copy-done.6
  37.4 0.1 broadcast_in_dim.2.screen_ref
  37.5 0.0 copy-done.3
  37.5 1.4 %coef.1.coef_ref = f32[8,8,128]{2,1,0:T(8,128)S(1)} custom-call(s32[2]{0:T(128)S(1)} %pad_add_fusion.where_ref, s32[3,8192]{1,0:T(4,128)S(1)} %copy-done.3, f32[32,128]{1,0:T(8,128)S(1)} %broadcast_in_dim.2.screen_ref, bf16[512,128]{1,0:T(8,128)(2,1)} %factor.1.after_ref), custom_call_target="tpu_custom_call" | custom-call | flops 268435456 | bytes 65536 | tf_op jit(solution)/shard_map/coef/pallas_call | solution.py:462
  38.9 0.0 collective-permute-done.g1_ref
  38.9 1.1 %all-to-all-done.1 = bf16[64,8,128]{2,1,0:T(8,128)(2,1)S(1)} async-done(((bf16[64,8,128]{2,1,0:T(8,128)(2,1)}), bf16[64,8,128]{2,1,0:T(8,128)(2,1)S(1)}, u32[]{:S(2)}, u32[]{:S(2)}) %all-to-all-start.1) | async-done | bytes 131104 | tf_op jit(solution)/shard_map/all_to_all | solution.py:407
  40.1 1.3 %owner.1 = (bf16[512,128]{1,0:T(8,128)(2,1)}, f32[40,128]{1,0:T(8,128)S(1)}) custom-call(s32[2]{0:T(128)S(1)} %pad_add_fusion.where_ref, bf16[512,128]{1,0:T(8,128)(2,1)S(1)} %bitcast.9, f32[8,8,128]{2,1,0:T(8,128)S(1)} %coef.1.coef_ref, f32[40,128]{1,0:T(8,128)S(1)} %get-tuple-element.12.step_ref, f32[40,128]{1,0:T(8,128)S(1)} %collective-permute-done.g1_ref), custom_call_target="tpu_custom_call" | custom-call | tf_op jit(solution)/shard_map/owner/pallas_call | solution.py:485
  41.4 10.1 %all-to-all-start.2 = ((bf16[64,8,128]{2,1,0:T(8,128)(2,1)}), bf16[64,8,128]{2,1,0:T(8,128)(2,1)S(1)}, u32[]{:S(2)}, u32[]{:S(2)}) async-start(bf16[64,8,128]{2,1,0:T(8,128)(2,1)} %bitcast.5), calls=%async_computation.2 | async-start | bytes 262144 | tf_op jit(solution)/shard_map/all_to_all | solution.py:407
  51.5 5.7 %collective-permute-start.1 = (f32[40,128]{1,0:T(8,128)S(1)}, f32[40,128]{1,0:T(8,128)S(1)}, u32[]{:S(2)}, u32[]{:S(2)}) collective-permute-start(f32[40,128]{1,0:T(8,128)S(1)} %get-tuple-element.13), channel_id=1, source_target_pairs={{0,480},{32,64},{64,32},{96,128},{128,96},{160,192},{192,160},{224... | collective-permute-start | bytes 61448 | tf_op jit(solution)/shard_map/ppermute | solution.py:494
  57.1 2.3 %own.1.own_ref = f32[32,1024]{1,0:T(8,128)S(1)} custom-call(s32[1]{0:T(128)S(6)} %copy.9.count_ref.refs_0_, f32[3,1024]{1,0:T(4,128)S(1)} %copy-done.1, bf16[32,1024]{1,0:T(8,128)(2,1)S(1)} %copy-done, bf16[512,128]{1,0:T(8,128)(2,1)} %get-tuple-element.14.after_ref), custom_call_target="tpu_custom_call" | custom-call | tf_op jit(solution)/shard_map/own/pallas_call | solution.py:495
  59.5 0.0 all-to-all-done.2
  59.5 3.9 %field.1.part_ref = f32[7,4,1024]{2,1,0:T(4,128)S(1)} custom-call(bf16[512,128]{1,0:T(8,128)(2,1)S(1)} %bitcast.7, s32[8,4,1024]{2,1,0:T(4,128)S(1)} %all_to_all.20.in_ref, f32[32,1024]{1,0:T(8,128)S(1)} %own.1.own_ref), custom_call_target="tpu_custom_call" | custom-call | tf_op jit(solution)/shard_map/field/pallas_call | solution.py:509
  63.4 0.0 collective-permute-done.1.g2_ref
  63.4 1.2 %rest.1.after_ref = f32[8,4,1024]{2,1,0:T(4,128)} custom-call(bf16[512,128]{1,0:T(8,128)(2,1)S(1)} %bitcast.8, s32[8,4,1024]{2,1,0:T(4,128)S(1)} %all_to_all.20.in_ref, f32[7,4,1024]{2,1,0:T(4,128)S(1)} %field.1.part_ref, f32[40,128]{1,0:T(8,128)S(1)} %collective-permute-done.1.g2_ref), custom_call_target="tpu_custom_call" | custom-call | tf_op jit(solution)/shard_map/rest/pallas_call | solution.py:518
  64.6 0.0 copy-start.4
  64.6 0.0 copy-start.5
  64.6 7.2 %all-to-all-start.3 = ((f32[8,4,1024]{2,1,0:T(4,128)}), f32[8,4,1024]{2,1,0:T(4,128)S(1)}, u32[]{:S(2)}, u32[]{:S(2)}) async-start(f32[8,4,1024]{2,1,0:T(4,128)} %rest.1.after_ref), calls=%async_computation.3 | async-start | bytes 262144 | tf_op jit(solution)/shard_map/all_to_all | solution.py:407
  71.8 0.0 copy-done.4
  71.8 0.0 copy-done.5
  71.8 1.0 %short.1 = (f32[32,1024]{1,0:T(8,128)S(1)}, bf16[32,64]{1,0:T(8,128)(2,1)S(1)}) custom-call(f32[3,1024]{1,0:T(4,128)S(1)} %copy-done.1, bf16[32,1024]{1,0:T(8,128)(2,1)S(1)} %copy-done, f32[40,128]{1,0:T(8,128)S(1)} %collective-permute-done.g1_ref, f32[40,128]{1,0:T(8,128)S(1)} %collective-permute-done.1.g2_ref, f32[32,1024]{1,0:T(8,128)S(1)} %own.1.own_ref, ...), custom_call_target="tpu_custom_call" | custom-call | flops 134217728 | bytes 327680 | tf_op jit(solution)/shard_map/short/pallas_call | solution.py:527
  72.8 1.5 %all-to-all-done.3 = f32[8,4,1024]{2,1,0:T(4,128)S(1)} async-done(((f32[8,4,1024]{2,1,0:T(4,128)}), f32[8,4,1024]{2,1,0:T(4,128)S(1)}, u32[]{:S(2)}, u32[]{:S(2)}) %all-to-all-start.3) | async-done | bytes 131104 | tf_op jit(solution)/shard_map/all_to_all | solution.py:407
  74.4 0.8 %final.1 = bf16[32,1024]{1,0:T(8,128)(2,1)} custom-call(s32[1]{0:T(128)S(6)} %copy.9.count_ref.refs_0_, f32[32,1024]{1,0:T(8,128)S(1)} %get-tuple-element.15.refs_1_, f32[32,1024]{1,0:T(8,128)S(1)} %reshape.24.refs_2_, bf16[32,64]{1,0:T(8,128)(2,1)S(1)} %get-tuple-element.16.refs_3_), custom_call_target="tpu_custom_call" | custom-call | tf_op jit(solution)/shard_map/final/pallas_call | solution.py:539
  (1 shorter events, 0.0 us)
Async XLA Ops:
  20.5 19.5 %all-to-all-start.1 = ((bf16[64,8,128]{2,1,0:T(8,128)(2,1)}), bf16[64,8,128]{2,1,0:T(8,128)(2,1)S(1)}, u32[]{:S(2)}, u32[]{:S(2)}) async-start(bf16[64,8,128]{2,1,0:T(8,128)(2,1)} %bitcast.3), calls=%async_computation.1 | async-start | bytes 262144 | tf_op jit(solution)/shard_map/all_to_all | solution.py:407
  33.2 0.8 %copy-start = (bf16[32,1024]{1,0:T(8,128)(2,1)S(1)}, bf16[32,1024]{1,0:T(8,128)(2,1)}, u32[]{:S(2)}) copy-start(bf16[32,1024]{1,0:T(8,128)(2,1)} %feat_ref.5) | copy-start | bytes 196612
  33.2 0.8 %copy-start.1 = (f32[3,1024]{1,0:T(4,128)S(1)}, f32[3,1024]{1,0:T(4,128)}, u32[]{:S(2)}) copy-start(f32[3,1024]{1,0:T(4,128)} %pos_ref.5) | copy-start | bytes 36868
  33.3 0.7 copy-start.2
  33.3 4.2 %copy-start.3 = (s32[3,8192]{1,0:T(4,128)S(1)}, s32[3,8192]{1,0:T(4,128)}, u32[]{:S(2)}) copy-start(s32[3,8192]{1,0:T(4,128)} %kvec_ref.1) | copy-start | bytes 294916
  34.2 3.2 %copy-start.6 = (f32[32]{0:T(128)S(1)}, f32[32]{0:T(128)}, u32[]{:S(2)}) copy-start(f32[32]{0:T(128)} %param.13) | copy-start | bytes 388
  34.2 4.7 %collective-permute-start = (f32[40,128]{1,0:T(8,128)S(1)}, f32[40,128]{1,0:T(8,128)S(1)}, u32[]{:S(2)}, u32[]{:S(2)}) collective-permute-start(f32[40,128]{1,0:T(8,128)S(1)} %get-tuple-element.11), channel_id=1, source_target_pairs={{0,32},{32,0},{64,96},{96,64},{128,160},{160,128},{192,224},{224,1... | collective-permute-start | bytes 61448 | tf_op jit(solution)/shard_map/ppermute | solution.py:484
  41.4 18.1 %all-to-all-start.2 = ((bf16[64,8,128]{2,1,0:T(8,128)(2,1)}), bf16[64,8,128]{2,1,0:T(8,128)(2,1)S(1)}, u32[]{:S(2)}, u32[]{:S(2)}) async-start(bf16[64,8,128]{2,1,0:T(8,128)(2,1)} %bitcast.5), calls=%async_computation.2 | async-start | bytes 262144 | tf_op jit(solution)/shard_map/all_to_all | solution.py:407
  51.5 11.9 %collective-permute-start.1 = (f32[40,128]{1,0:T(8,128)S(1)}, f32[40,128]{1,0:T(8,128)S(1)}, u32[]{:S(2)}, u32[]{:S(2)}) collective-permute-start(f32[40,128]{1,0:T(8,128)S(1)} %get-tuple-element.13), channel_id=1, source_target_pairs={{0,480},{32,64},{64,32},{96,128},{128,96},{160,192},{192,160},{224... | collective-permute-start | bytes 61448 | tf_op jit(solution)/shard_map/ppermute | solution.py:494
  64.6 7.2 %copy-start.4 = (bf16[32,32]{1,0:T(8,128)(2,1)S(1)}, bf16[32,32]{1,0:T(8,128)(2,1)}, u32[]{:S(2)}) copy-start(bf16[32,32]{1,0:T(8,128)(2,1)} %lw_ref.1) | copy-start | bytes 6148
  64.6 7.2 %copy-start.5 = (bf16[32,32]{1,0:T(8,128)(2,1)S(1)}, bf16[32,32]{1,0:T(8,128)(2,1)}, u32[]{:S(2)}) copy-start(bf16[32,32]{1,0:T(8,128)(2,1)} %sw_ref.1) | copy-start | bytes 6148
  64.6 9.7 %all-to-all-start.3 = ((f32[8,4,1024]{2,1,0:T(4,128)}), f32[8,4,1024]{2,1,0:T(4,128)S(1)}, u32[]{:S(2)}, u32[]{:S(2)}) async-start(f32[8,4,1024]{2,1,0:T(4,128)} %rest.1.after_ref), calls=%async_computation.3 | async-start | bytes 262144 | tf_op jit(solution)/shard_map/all_to_all | solution.py:407

commit v6 on v5

--- a/solution.py
+++ b/solution.py
@@ -308,7 +308,7 @@
         out_ref[16 * n : 16 * n + 16, :] = twice
 
 
-def field_blocks(first, filt_ref, in_ref, out_ref, e_ref, g_ref, turns_ref):
+def field_blocks(first, last, filt_ref, in_ref, e_ref, g_ref, turns_ref):
     unpack_turns(in_ref, turns_ref)
     rows = filt_ref.shape[0]
     late = 8 * (first_out - first_in) % rows
@@ -316,8 +316,9 @@
         g_ref[late:rows, at : at + 128] = filt_ref[0 : rows - late, :]
         if late:
             g_ref[0:late, at : at + 128] = filt_ref[rows - late : rows, :]
-    atoms = out_ref.shape[2]
-    for k in range(first, out_ref.shape[0]):
+    atoms = in_ref.shape[2]
+    found = []
+    for k in range(first, last):
         cols = slice((k - first) * atoms, (k - first + 1) * atoms)
         ytab = table(turns_ref[1, k : k + 1, :], "y")
         store_wide(turns_ref[0, k : k + 1, :], ytab, e_ref, cols)
@@ -329,19 +330,21 @@
             for n in range(1, 16):
                 acc = acc + term[128 * c + 8 * n : 128 * c + 8 * n + 8] * groups[n]
             lines.append(jnp.sum(acc, axis=0, keepdims=True))
-        out_ref[k] = jnp.concatenate(lines, axis=0)
+        found.append(jnp.concatenate(lines, axis=0))
+    return found
 
 
 def field_kernel(filt_ref, in_ref, own_ref, out_ref, e_ref, g_ref, turns_ref):
     del own_ref
-    field_blocks(0, filt_ref, in_ref, out_ref, e_ref, g_ref, turns_ref)
+    for k, lines in enumerate(field_blocks(0, out_ref.shape[0], filt_ref, in_ref, e_ref, g_ref, turns_ref)):
+        out_ref[k] = lines
 
 
 def rest_kernel(filt_ref, in_ref, part_ref, g2_ref, out_ref, e_ref, g_ref, turns_ref):
     del g2_ref
     done = part_ref.shape[0]
-    out_ref[0:done] = part_ref[...]
-    field_blocks(done, filt_ref, in_ref, out_ref, e_ref, g_ref, turns_ref)
+    found = field_blocks(done, in_ref.shape[0], filt_ref, in_ref, e_ref, g_ref, turns_ref)
+    out_ref[...] = jnp.concatenate([part_ref[k] for k in range(done)] + found, axis=0).astype(bf16)
 
 
 shrink = math.sqrt(math.log2(math.e) / pair_scale)
@@ -396,7 +399,7 @@
 
 
 def final_kernel(count_ref, base_ref, long_ref, twice_ref, out_ref, *, long_scale):
-    mixed = jnp.dot(twice_ref[...], split(long_ref[...]), preferred_element_type=f32)
+    mixed = jnp.dot(twice_ref[...], split(long_ref[...].astype(f32)), preferred_element_type=f32)
     total = base_ref[...] + long_scale * mixed
     out_ref[...] = (total * valid_row(count_ref, total.shape[1])).astype(bf16)
 
@@ -518,7 +521,7 @@
     field = pl.pallas_call(
         rest_kernel,
         name="rest",
-        out_shape=jax.ShapeDtypeStruct((near, 4, atoms), f32),
+        out_shape=jax.ShapeDtypeStruct((chans, atoms), bf16),
         in_specs=[whole()] * 3 + [whole(pl.ANY)],
         out_specs=whole(),
         scratch_shapes=field_scratch,
@@ -533,7 +536,7 @@
         compiler_params=params,
         cost_estimate=pl.CostEstimate(flops=2 * 256 * 256 * atoms, bytes_accessed=10 * 32 * atoms, transcendentals=256 * atoms),
     )(positions, features, ghosts_1, ghosts_2, own, long_weight, short_weight, field)
-    longmsg = swap_parts(field, NEAR, first_near).reshape(chans, atoms)
+    longmsg = swap_parts(field.reshape(near, 4, atoms), NEAR, first_near).reshape(chans, atoms)
     all_atoms = atoms * lax.axis_size(ALL)
     long_scale = long_gain / math.sqrt(total_vec * all_atoms)
     return pl.pallas_call(

time: 75.7 us -> 75.4 us (level)
  no operation moved by 1% of the time
where the time goes in v6:
time: 75.4 us; the launch traced here: 74.8 us
  starting transfers between devices  38.7 us (51%)
  Pallas kernels  17.4 us (23%)
  blocking collectives  13.9 us (18%)
  waiting for transfers between devices  2.36 us (3%)
  local copies, waits for them, and re-layouts  1.49 us (2%)
  between operations  0.82 us (1%)
    all_to_all x3, starting transfers between devices, swap_parts(): lax.all_to_all(parts, axis, 0, 0, axis_index_groups=order, tiled=True)  29.9 us
    all_to_all x1, blocking collectives, swap_parts(): lax.all_to_all(parts, axis, 0, 0, axis_index_groups=order, tiled=True)  13.9 us
    ppermute x1, starting transfers between devices, local(): ghosts_2 = lax.ppermute(step_face, DOM, step)  5.66 us
    pallas_call x1, Pallas kernels, local(): pl.pallas_call(factor_kernel, name='factor', out_shape=rows, in_specs=[wh...  4.39 us
    pallas_call x1, Pallas kernels, local(): pl.pallas_call(field_kernel, name='field', out_shape=jax.ShapeDtypeStruct...  3.88 us
    ppermute x1, starting transfers between devices, local(): ghosts_1 = lax.ppermute(flip_face, DOM, flip)  3.18 us
    all_to_all x3, waiting for transfers between devices, swap_parts(): lax.all_to_all(parts, axis, 0, 0, axis_index_groups=order, tiled=True)  2.35 us
    pallas_call x1, Pallas kernels, local(): pl.pallas_call(own_kernel, name='own', out_shape=jax.ShapeDtypeStruct((ch...  2.35 us
  transfers between devices with their start and end apart: 5, of which 2 were waited for; matrix products, arithmetic and copies ran while one was open for 0% of the time, Pallas kernels for 12%

profile of v6, /device:TPU:1, one launch (start us, length us, event | category | flops | bytes accessed | tf_op | source)
XLA Modules:
  0.0 74.8 jit_solution(6558669724888843517)
XLA Ops:
  0.7 1.6 %prep.1 = s32[8,4,1024]{2,1,0:T(4,128)} custom-call(s32[1]{0:T(128)S(6)} %copy.9.count_ref.refs_0_, f32[3,1024]{1,0:T(4,128)} %pos_ref.5, bf16[32,1024]{1,0:T(8,128)(2,1)} %feat_ref.5), custom_call_target="tpu_custom_call" | custom-call | tf_op jit(solution)/shard_map/prep/pallas_call | solution.py:425
  2.3 13.9 %all_to_all.20.in_ref = s32[8,4,1024]{2,1,0:T(4,128)S(1)} all-to-all(s32[8,4,1024]{2,1,0:T(4,128)} %prep.1), channel_id=1, replica_groups={{256,288,384,416,0,32,128,160},{257,289,385,417,1,33,129,161},{258,290,..., dimensions={0} | all-to-all | bytes 262144 | tf_op jit(solution)/shard_map/all_to_all | solution.py:410
  16.1 4.4 %factor.1.after_ref = bf16[512,128]{1,0:T(8,128)(2,1)} custom-call(s32[8,4,1024]{2,1,0:T(4,128)S(1)} %all_to_all.20.in_ref), custom_call_target="tpu_custom_call" | custom-call | tf_op jit(solution)/shard_map/factor/pallas_call | solution.py:445
  20.5 12.6 %all-to-all-start.1 = ((bf16[64,8,128]{2,1,0:T(8,128)(2,1)}), bf16[64,8,128]{2,1,0:T(8,128)(2,1)S(1)}, u32[]{:S(2)}, u32[]{:S(2)}) async-start(bf16[64,8,128]{2,1,0:T(8,128)(2,1)} %bitcast.3), calls=%async_computation.1 | async-start | bytes 262144 | tf_op jit(solution)/shard_map/all_to_all | solution.py:410
  33.2 0.0 copy-start
  33.2 0.0 copy-start.1
  33.2 0.1 pad_add_fusion.where_ref
  33.3 0.0 copy-start.2
  33.3 0.0 copy-start.3
  33.3 0.7 copy-done
  34.0 0.0 copy-done.1
  34.0 0.0 copy-done.2
  34.0 0.2 faces.1
  34.2 0.0 copy-start.6
  34.2 3.2 %collective-permute-start = (f32[40,128]{1,0:T(8,128)S(1)}, f32[40,128]{1,0:T(8,128)S(1)}, u32[]{:S(2)}, u32[]{:S(2)}) collective-permute-start(f32[40,128]{1,0:T(8,128)S(1)} %get-tuple-element.11), channel_id=1, source_target_pairs={{0,32},{32,0},{64,96},{96,64},{128,160},{160,128},{192,224},{224,1... | collective-permute-start | bytes 61448 | tf_op jit(solution)/shard_map/ppermute | solution.py:487
  37.4 0.0 copy-done.6
  37.4 0.1 broadcast_in_dim.2.screen_ref
  37.5 0.0 copy-done.3
  37.5 1.4 %coef.1.coef_ref = f32[8,8,128]{2,1,0:T(8,128)S(1)} custom-call(s32[2]{0:T(128)S(1)} %pad_add_fusion.where_ref, s32[3,8192]{1,0:T(4,128)S(1)} %copy-done.3, f32[32,128]{1,0:T(8,128)S(1)} %broadcast_in_dim.2.screen_ref, bf16[512,128]{1,0:T(8,128)(2,1)} %factor.1.after_ref), custom_call_target="tpu_custom_call" | custom-call | flops 268435456 | bytes 65536 | tf_op jit(solution)/shard_map/coef/pallas_call | solution.py:465
  38.9 0.0 collective-permute-done.g1_ref
  38.9 1.1 %all-to-all-done.1 = bf16[64,8,128]{2,1,0:T(8,128)(2,1)S(1)} async-done(((bf16[64,8,128]{2,1,0:T(8,128)(2,1)}), bf16[64,8,128]{2,1,0:T(8,128)(2,1)S(1)}, u32[]{:S(2)}, u32[]{:S(2)}) %all-to-all-start.1) | async-done | bytes 131104 | tf_op jit(solution)/shard_map/all_to_all | solution.py:410
  40.1 1.3 %owner.1 = (bf16[512,128]{1,0:T(8,128)(2,1)}, f32[40,128]{1,0:T(8,128)S(1)}) custom-call(s32[2]{0:T(128)S(1)} %pad_add_fusion.where_ref, bf16[512,128]{1,0:T(8,128)(2,1)S(1)} %bitcast.9, f32[8,8,128]{2,1,0:T(8,128)S(1)} %coef.1.coef_ref, f32[40,128]{1,0:T(8,128)S(1)} %get-tuple-element.12.step_ref, f32[40,128]{1,0:T(8,128)S(1)} %collective-permute-done.g1_ref), custom_call_target="tpu_custom_call" | custom-call | tf_op jit(solution)/shard_map/owner/pallas_call | solution.py:488
  41.4 10.1 %all-to-all-start.2 = ((bf16[64,8,128]{2,1,0:T(8,128)(2,1)}), bf16[64,8,128]{2,1,0:T(8,128)(2,1)S(1)}, u32[]{:S(2)}, u32[]{:S(2)}) async-start(bf16[64,8,128]{2,1,0:T(8,128)(2,1)} %bitcast.5), calls=%async_computation.2 | async-start | bytes 262144 | tf_op jit(solution)/shard_map/all_to_all | solution.py:410
  51.5 5.7 %collective-permute-start.1 = (f32[40,128]{1,0:T(8,128)S(1)}, f32[40,128]{1,0:T(8,128)S(1)}, u32[]{:S(2)}, u32[]{:S(2)}) collective-permute-start(f32[40,128]{1,0:T(8,128)S(1)} %get-tuple-element.13), channel_id=1, source_target_pairs={{0,480},{32,64},{64,32},{96,128},{128,96},{160,192},{192,160},{224... | collective-permute-start | bytes 61448 | tf_op jit(solution)/shard_map/ppermute | solution.py:497
  57.1 2.3 %own.1.own_ref = f32[32,1024]{1,0:T(8,128)S(1)} custom-call(s32[1]{0:T(128)S(6)} %copy.9.count_ref.refs_0_, f32[3,1024]{1,0:T(4,128)S(1)} %copy-done.1, bf16[32,1024]{1,0:T(8,128)(2,1)S(1)} %copy-done, bf16[512,128]{1,0:T(8,128)(2,1)} %get-tuple-element.14.after_ref), custom_call_target="tpu_custom_call" | custom-call | tf_op jit(solution)/shard_map/own/pallas_call | solution.py:498
  59.5 0.0 all-to-all-done.2
  59.5 3.9 %field.1.part_ref = f32[7,4,1024]{2,1,0:T(4,128)S(1)} custom-call(bf16[512,128]{1,0:T(8,128)(2,1)S(1)} %bitcast.7, s32[8,4,1024]{2,1,0:T(4,128)S(1)} %all_to_all.20.in_ref, f32[32,1024]{1,0:T(8,128)S(1)} %own.1.own_ref), custom_call_target="tpu_custom_call" | custom-call | tf_op jit(solution)/shard_map/field/pallas_call | solution.py:512
  63.4 0.0 collective-permute-done.1.g2_ref
  63.4 0.6 rest.1.after_ref
  64.0 0.7 reshape.27
  64.6 0.0 copy-start.4
  64.6 0.0 copy-start.5
  64.6 7.2 %all-to-all-start.3 = ((bf16[8,4,1024]{2,1,0:T(4,128)(2,1)}), bf16[8,4,1024]{2,1,0:T(4,128)(2,1)S(1)}, u32[]{:S(2)}, u32[]{:S(2)}) async-start(bf16[8,4,1024]{2,1,0:T(4,128)(2,1)} %reshape.27), calls=%async_computation.3 | async-start | bytes 131072 | tf_op jit(solution)/shard_map/all_to_all | solution.py:410
  71.8 0.0 copy-done.4
  71.8 0.0 copy-done.5
  71.8 1.0 %short.1 = (f32[32,1024]{1,0:T(8,128)S(1)}, bf16[32,64]{1,0:T(8,128)(2,1)S(1)}) custom-call(f32[3,1024]{1,0:T(4,128)S(1)} %copy-done.1, bf16[32,1024]{1,0:T(8,128)(2,1)S(1)} %copy-done, f32[40,128]{1,0:T(8,128)S(1)} %collective-permute-done.g1_ref, f32[40,128]{1,0:T(8,128)S(1)} %collective-permute-done.1.g2_ref, f32[32,1024]{1,0:T(8,128)S(1)} %own.1.own_ref, ...), custom_call_target="tpu_custom_call" | custom-call | flops 134217728 | bytes 327680 | tf_op jit(solution)/shard_map/short/pallas_call | solution.py:530
  72.8 1.2 %all-to-all-done.3 = bf16[8,4,1024]{2,1,0:T(4,128)(2,1)S(1)} async-done(((bf16[8,4,1024]{2,1,0:T(4,128)(2,1)}), bf16[8,4,1024]{2,1,0:T(4,128)(2,1)S(1)}, u32[]{:S(2)}, u32[]{:S(2)}) %all-to-all-start.3) | async-done | bytes 65568 | tf_op jit(solution)/shard_map/all_to_all | solution.py:410
  74.0 0.8 %final.1 = bf16[32,1024]{1,0:T(8,128)(2,1)} custom-call(s32[1]{0:T(128)S(6)} %copy.9.count_ref.refs_0_, f32[32,1024]{1,0:T(8,128)S(1)} %get-tuple-element.15.refs_1_, bf16[32,1024]{1,0:T(8,128)(2,1)S(1)} %reshape.28.refs_2_, bf16[32,64]{1,0:T(8,128)(2,1)S(1)} %get-tuple-element.16.refs_3_), custom_call_target="tpu_custom_call" | custom-call | tf_op jit(solution)/shard_map/final/pallas_call | solution.py:542
  (1 shorter events, 0.0 us)
Async XLA Ops:
  20.5 19.5 %all-to-all-start.1 = ((bf16[64,8,128]{2,1,0:T(8,128)(2,1)}), bf16[64,8,128]{2,1,0:T(8,128)(2,1)S(1)}, u32[]{:S(2)}, u32[]{:S(2)}) async-start(bf16[64,8,128]{2,1,0:T(8,128)(2,1)} %bitcast.3), calls=%async_computation.1 | async-start | bytes 262144 | tf_op jit(solution)/shard_map/all_to_all | solution.py:410
  33.2 0.8 %copy-start = (bf16[32,1024]{1,0:T(8,128)(2,1)S(1)}, bf16[32,1024]{1,0:T(8,128)(2,1)}, u32[]{:S(2)}) copy-start(bf16[32,1024]{1,0:T(8,128)(2,1)} %feat_ref.5) | copy-start | bytes 196612
  33.2 0.8 %copy-start.1 = (f32[3,1024]{1,0:T(4,128)S(1)}, f32[3,1024]{1,0:T(4,128)}, u32[]{:S(2)}) copy-start(f32[3,1024]{1,0:T(4,128)} %pos_ref.5) | copy-start | bytes 36868
  33.3 0.7 copy-start.2
  33.3 4.2 %copy-start.3 = (s32[3,8192]{1,0:T(4,128)S(1)}, s32[3,8192]{1,0:T(4,128)}, u32[]{:S(2)}) copy-start(s32[3,8192]{1,0:T(4,128)} %kvec_ref.1) | copy-start | bytes 294916
  34.2 3.2 %copy-start.6 = (f32[32]{0:T(128)S(1)}, f32[32]{0:T(128)}, u32[]{:S(2)}) copy-start(f32[32]{0:T(128)} %param.13) | copy-start | bytes 388
  34.2 4.7 %collective-permute-start = (f32[40,128]{1,0:T(8,128)S(1)}, f32[40,128]{1,0:T(8,128)S(1)}, u32[]{:S(2)}, u32[]{:S(2)}) collective-permute-start(f32[40,128]{1,0:T(8,128)S(1)} %get-tuple-element.11), channel_id=1, source_target_pairs={{0,32},{32,0},{64,96},{96,64},{128,160},{160,128},{192,224},{224,1... | collective-permute-start | bytes 61448 | tf_op jit(solution)/shard_map/ppermute | solution.py:487
  41.4 18.1 %all-to-all-start.2 = ((bf16[64,8,128]{2,1,0:T(8,128)(2,1)}), bf16[64,8,128]{2,1,0:T(8,128)(2,1)S(1)}, u32[]{:S(2)}, u32[]{:S(2)}) async-start(bf16[64,8,128]{2,1,0:T(8,128)(2,1)} %bitcast.5), calls=%async_computation.2 | async-start | bytes 262144 | tf_op jit(solution)/shard_map/all_to_all | solution.py:410
  51.5 11.9 %collective-permute-start.1 = (f32[40,128]{1,0:T(8,128)S(1)}, f32[40,128]{1,0:T(8,128)S(1)}, u32[]{:S(2)}, u32[]{:S(2)}) collective-permute-start(f32[40,128]{1,0:T(8,128)S(1)} %get-tuple-element.13), channel_id=1, source_target_pairs={{0,480},{32,64},{64,32},{96,128},{128,96},{160,192},{192,160},{224... | collective-permute-start | bytes 61448 | tf_op jit(solution)/shard_map/ppermute | solution.py:497
  64.6 7.2 %copy-start.4 = (bf16[32,32]{1,0:T(8,128)(2,1)S(1)}, bf16[32,32]{1,0:T(8,128)(2,1)}, u32[]{:S(2)}) copy-start(bf16[32,32]{1,0:T(8,128)(2,1)} %lw_ref.1) | copy-start | bytes 6148
  64.6 7.2 %copy-start.5 = (bf16[32,32]{1,0:T(8,128)(2,1)S(1)}, bf16[32,32]{1,0:T(8,128)(2,1)}, u32[]{:S(2)}) copy-start(bf16[32,32]{1,0:T(8,128)(2,1)} %sw_ref.1) | copy-start | bytes 6148
  64.6 9.4 %all-to-all-start.3 = ((bf16[8,4,1024]{2,1,0:T(4,128)(2,1)}), bf16[8,4,1024]{2,1,0:T(4,128)(2,1)S(1)}, u32[]{:S(2)}, u32[]{:S(2)}) async-start(bf16[8,4,1024]{2,1,0:T(4,128)(2,1)} %reshape.27), calls=%async_computation.3 | async-start | bytes 131072 | tf_op jit(solution)/shard_map/all_to_all | solution.py:410
